TPU v7x, 32 devices: a whole 2x2x4 slice. The times are simulated.
32 devices in a mesh: strip: 8 (over z, x), cells: 4 (over y, core).
Axes of the slice: x: 2, y: 2, z: 4, core: 2. Of those that a mesh axis runs over, the one named last changes fastest.
Arguments:
- pin_rows: int32 [131072], P(('strip', 'cells')), may hold values from 0 to 2
- pin_cols: int32 [131072], P(('strip', 'cells')), may hold values from 0 to 2558
- pin_fracs: float32 [2, 131072], P(None, ('strip', 'cells')), may hold values from 0 to 1
- pin_weights: float32 [131072], P(('strip', 'cells')), may hold values from 0.5 to 1.5
- capacity: int32 [32, 2560], P('strip', 'cells'), may hold values from 1 to 4
- blockage: float32 [32, 2560], P('strip', 'cells'), may hold values from 0 to 0.5
- row_blocks: float32 [20, 128, 128], P('cells'), may hold values from -0.002 to 0.15
- col_blocks: float32 [1, 32, 32], replicated, may hold values from -0.002 to 0.15
Outputs:
- final_density: float32 [32, 2560], P('strip', 'cells')
- pin_velocity: float32 [2, 131072], P(None, ('strip', 'cells'))
All inputs are finite; a program needn't handle non-finite values.
Results may differ from a plain program's by a relative error of at most 0.0052.
Values may be sent and summed in bfloat16 or wider, within the bound.
No kernel may reach another device: no remote copies, remote signals or barrier semaphores. Data moves between devices by JAX's collectives and lax.ppermute only.
A program may use at most 64 MiB of HBM per device.

v0:
```python
import jax
import jax.numpy as jnp
from jax import lax
from jax.sharding import PartitionSpec as P

SWEEPS = 3
STEPS = 2


coupling = 2.0
floor_level = 0.5
highest = lax.Precision.HIGHEST


def padded_2(block, sides, width):
    for axis, dim in sides:
        count = lax.axis_size(axis)
        forward = [(i, i + 1) for i in range(count - 1)]
        backward = [(target, source) for source, target in forward]
        low = lax.ppermute(
            lax.slice_in_dim(block, block.shape[dim] - width, None, axis=dim), axis, forward
        )
        high = lax.ppermute(lax.slice_in_dim(block, 0, width, axis=dim), axis, backward)
        block = jnp.concatenate([low, block, high], axis=dim)
    return block


def along_lines(values):
    padded = jnp.pad(values, ((0, 0), (1, 1)), mode="edge")
    return 2.0 * values - padded[:, :-2] - padded[:, 2:]


def blockwise(residual, blocks):
    leading = residual.shape[0]
    pieces = residual.reshape(leading, blocks.shape[0], blocks.shape[1])
    result = jnp.einsum("rnj,nij->rni", pieces, blocks, precision=highest)
    return result.reshape(leading, blocks.shape[0] * blocks.shape[1])


def line_solve(source, weights, start_iterate, blocks):
    iterate = start_iterate
    for sweep_index in range(SWEEPS):
        residual = source - (weights * iterate + coupling * along_lines(iterate))
        iterate = iterate + blockwise(residual, blocks)
    return iterate


def vertical_rims(values, padded):
    at_first = lax.axis_index("strip") == 0
    at_last = lax.axis_index("strip") == lax.axis_size("strip") - 1
    upper_rim = jnp.where(at_first, values[:1], padded[:1])
    lower_rim = jnp.where(at_last, values[-1:], padded[-1:])
    row_above = jnp.concatenate([upper_rim, values[:-1]], 0)
    row_below = jnp.concatenate([values[1:], lower_rim], 0)
    return (row_above, row_below)


def horizontal_rims(values, padded):
    at_first = lax.axis_index("cells") == 0
    at_last = lax.axis_index("cells") == lax.axis_size("cells") - 1
    left_rim = jnp.where(at_first, values[:, :1], padded[:, :1])
    right_rim = jnp.where(at_last, values[:, -1:], padded[:, -1:])
    left_cells = jnp.concatenate([left_rim, values[:, :-1]], 1)
    right_cells = jnp.concatenate([values[:, 1:], right_rim], 1)
    return (left_cells, right_cells)


def row_lines(values):
    padded = padded_2(values, (("cells", 1),), 1)
    left_cells, right_cells = horizontal_rims(values, padded)
    return 2.0 * values - left_cells - right_cells


def row_solve(source, weights, start_iterate, blocks):
    iterate = start_iterate
    for sweep_index in range(SWEEPS):
        residual = source - (weights * iterate + coupling * row_lines(iterate))
        iterate = iterate + blockwise(residual, blocks)
    return iterate


def pin_tables(block_rows, block_cols, row_near, row_far, col_near, col_far, rows_dev, hi_count):
    block_size = block_rows.shape[0]
    zero_value = jnp.zeros((), jnp.bfloat16)
    row_index = lax.broadcasted_iota(jnp.int32, (block_size, rows_dev), 1)
    row_table = jnp.where(
        row_index == block_rows[:, None], row_near[:, None], zero_value
    ) + jnp.where(row_index == block_rows[:, None] + 1, row_far[:, None], zero_value)
    high_index = lax.broadcasted_iota(jnp.int32, (block_size, 1, hi_count), 2)
    low_index = lax.broadcasted_iota(jnp.int32, (block_size, 128), 1)
    bin_tables = []
    lane_tables = []
    for offset, factor in ((0, col_near), (1, col_far)):
        column = block_cols + offset
        high_part = column // 128
        low_part = column - high_part * 128
        chosen = (high_index == high_part[:, None, None]).astype(jnp.bfloat16)
        bin_tables.append((row_table[:, :, None] * chosen).reshape(block_size, rows_dev * hi_count))
        lane_tables.append(jnp.where(low_index == low_part[:, None], factor[:, None], zero_value))
    return (jnp.concatenate(bin_tables, 0), jnp.concatenate(lane_tables, 0))


def pin_factors(pin_rows, pin_cols, row_near, row_far, col_near, col_far):
    block_size = min(2048, pin_rows.shape[0])
    return (
        block_size,
        tuple(
            (
                item.reshape(-1, block_size)
                for item in (pin_rows, pin_cols, row_near, row_far, col_near, col_far)
            )
        ),
    )


def splat(pin_rows, pin_cols, pin_fracs, pin_weights, rows_dev, hi_count):
    near_y = 1.0 - pin_fracs[0]
    near_x = 1.0 - pin_fracs[1]
    block_size, pieces = pin_factors(
        pin_rows,
        pin_cols,
        (pin_weights * near_y).astype(jnp.bfloat16),
        (pin_weights * pin_fracs[0]).astype(jnp.bfloat16),
        near_x.astype(jnp.bfloat16),
        pin_fracs[1].astype(jnp.bfloat16),
    )

    def add_block(total, block):
        bins, lane_table = pin_tables(
            block[0], block[1], block[2], block[3], block[4], block[5], rows_dev, hi_count
        )
        part_sum = lax.dot_general(
            bins, lane_table, (((0,), (0,)), ((), ())), preferred_element_type=jnp.float32
        )
        return (total + part_sum, None)

    total, unused = lax.scan(add_block, jnp.zeros((rows_dev * hi_count, 128), jnp.float32), pieces)
    return total.reshape(rows_dev, hi_count * 128)


def interpolate(pin_rows, pin_cols, pin_fracs, velocity_y, velocity_x, rows_dev, hi_count):
    stacked = jnp.concatenate(
        [
            velocity_y.reshape(rows_dev * hi_count, 128),
            velocity_x.reshape(rows_dev * hi_count, 128),
        ],
        1,
    )
    npins = pin_rows.shape[0]
    block_size, pieces = pin_factors(
        pin_rows,
        pin_cols,
        (1.0 - pin_fracs[0]).astype(jnp.bfloat16),
        pin_fracs[0].astype(jnp.bfloat16),
        (1.0 - pin_fracs[1]).astype(jnp.bfloat16),
        pin_fracs[1].astype(jnp.bfloat16),
    )

    def one_block(carry, block):
        bins, lane_table = pin_tables(
            block[0], block[1], block[2], block[3], block[4], block[5], rows_dev, hi_count
        )
        sampled = jnp.dot(bins, stacked, preferred_element_type=jnp.float32)
        lane_values = lane_table.astype(jnp.float32)
        both_y = jnp.sum(sampled[:, :128] * lane_values, axis=1)
        both_x = jnp.sum(sampled[:, 128:] * lane_values, axis=1)
        result = jnp.stack(
            [both_y[:block_size] + both_y[block_size:], both_x[:block_size] + both_x[block_size:]]
        )
        return (carry, result)

    unused, outputs = lax.scan(one_block, jnp.zeros((), jnp.float32), pieces)
    return jnp.transpose(outputs, (1, 0, 2)).reshape(2, npins)


def velocity_of(centre, left_cells, right_cells, row_above, row_below):
    scale = jnp.maximum(centre, floor_level)
    velocity_x = (-(0.5 * (right_cells - left_cells)) / scale).astype(jnp.bfloat16)
    velocity_y = (-(0.5 * (row_below - row_above)) / scale).astype(jnp.bfloat16)
    return (velocity_y, velocity_x)


def to_rows_middle(source_col, current_col):
    source_back, current_back = (
        lax.all_to_all(source_col, "strip", split_axis=1, concat_axis=0, tiled=True),
        lax.all_to_all(current_col, "strip", split_axis=1, concat_axis=0, tiled=True),
    )
    return (source_back.T, current_back.T)


def local(pin_rows, pin_cols, pin_fracs, pin_weights, capacity, blockage, row_blocks, col_blocks):
    rows_dev, cols_dev = capacity.shape
    hi_count = cols_dev * lax.axis_size("cells") // 128
    cap_weight = capacity.astype(jnp.float32) * (1.0 - blockage)
    partial_value = splat(pin_rows, pin_cols, pin_fracs, pin_weights, rows_dev, hi_count)
    whole = lax.psum(partial_value, "cells")
    density = lax.dynamic_slice_in_dim(whole, lax.axis_index("cells") * cols_dev, cols_dev, 1)
    current = density / cap_weight
    row_above, row_below = vertical_rims(current, padded_2(current, (("strip", 0),), 1))
    source = cap_weight * current - coupling * (2.0 * current - row_above - row_below)
    column_weight = cap_weight.T
    for step_index in range(STEPS):
        current = row_solve(source, cap_weight, current, row_blocks)
        middle = cap_weight * current - coupling * row_lines(current)
        if step_index == 0:
            middle_col, current_col, column_weight = (
                lax.all_to_all(middle.T, "strip", split_axis=0, concat_axis=1, tiled=True),
                lax.all_to_all(current.T, "strip", split_axis=0, concat_axis=1, tiled=True),
                lax.all_to_all(cap_weight.T, "strip", split_axis=0, concat_axis=1, tiled=True),
            )
        else:
            middle_col, current_col = (
                lax.all_to_all(middle.T, "strip", split_axis=0, concat_axis=1, tiled=True),
                lax.all_to_all(current.T, "strip", split_axis=0, concat_axis=1, tiled=True),
            )
        current_col = line_solve(middle_col, column_weight, current_col, col_blocks)
        if step_index + 1 < STEPS:
            source_col = column_weight * current_col - coupling * along_lines(current_col)
            source, current = to_rows_middle(source_col, current_col)
        else:
            current = lax.all_to_all(
                current_col, "strip", split_axis=1, concat_axis=0, tiled=True
            ).T
    padded = padded_2(current, (("strip", 0),), 1)
    row_above, row_below = vertical_rims(current, padded)
    extended = jnp.concatenate([row_above[:1], current, row_below[-1:]], 0)
    strip_field = lax.all_gather(extended, "cells", axis=1, tiled=True)
    centre = strip_field[1:-1]
    padded_cols = jnp.pad(centre, ((0, 0), (1, 1)), mode="edge")
    velocity_y, velocity_x = velocity_of(
        centre, padded_cols[:, :-2], padded_cols[:, 2:], strip_field[:-2], strip_field[2:]
    )
    pin_velocity = interpolate(
        pin_rows, pin_cols, pin_fracs, velocity_y, velocity_x, rows_dev, hi_count
    )
    return (current, pin_velocity)


def solution(mesh):
    placed = (
        P(("strip", "cells")),
        P(("strip", "cells")),
        P(None, ("strip", "cells")),
        P(("strip", "cells")),
        P("strip", "cells"),
        P("strip", "cells"),
        P("cells", None, None),
        P(),
    )
    return jax.shard_map(
        local,
        mesh=mesh,
        in_specs=placed,
        out_specs=(P("strip", "cells"), P(None, ("strip", "cells"))),
        check_vma=False,
    )
```

profile of v0, /device:TPU:0, one launch (start us, length us, event | category | flops | bytes accessed | tf_op | source)
XLA Modules:
  0.0 182.9 jit_solution(781674462339967463)
XLA Ops:
  4.7 4.6 %while.28 = (s32[]{:T(128)}, f32[80,128]{1,0:T(8,128)S(1)}, s32[2,2048]{1,0:T(2,128)S(1)}, bf16[2,2048]{1,0:T(2,128)(2,1)S(1)}, bf16[2,2048]{1,0:T(2,128)(2,1)S(...) while((s32[]{:T(128)}, f32[80,128]{1,0:T(8,128)S(1)}, ...), condition=%wide.region_1.2_spmd.clone, body=%wide.region_0.1_spmd.clone.sunk | while | flops 88993792 | bytes 5349499 | solution.py:137
  9.4 13.2 %psum.7 = f32[4,2560]{1,0:T(4,128)S(1)} all-reduce(f32[4,2560]{1,0:T(4,128)S(1)} %reshape.772), channel_id=1, replica_groups=mesh['strip'=8,'cells'=4] {'cells'}, use_global_device_ids=true, to_apply=%region_2.3 | all-reduce | flops 10240 | bytes 81920 | tf_op jit(solution)/shard_map/psum | solution.py:196
  22.6 3.4 %collective-permute-start = (f32[1,640]{1,0:T(1,128)S(1)}, f32[1,640]{1,0:T(1,128)S(1)}, u32[]{:S(2)}, u32[]{:S(2)}) collective-permute-start(f32[1,640]{1,0:T(1,128)S(1)} %get-tuple-element.440), channel_id=1, source_target_pairs={{0,4},{4,8},{8,12},{12,16},{16,20},{20,24},{24,28},{1,5},{5,9},{9,... | collective-permute-start | bytes 7688 | tf_op jit(solution)/shard_map/ppermute | solution.py:20
  30.7 7.0 %all-to-all-start.2 = ((f32[8,80,4]{1,2,0:T(4,128)}), f32[8,80,4]{1,2,0:T(4,128)S(1)}, u32[]{:S(2)}, u32[]{:S(2)}) async-start(f32[8,80,4]{1,2,0:T(4,128)} %copy.30), calls=%async_computation.2 | async-start | bytes 32768 | tf_op jit(solution)/shard_map/all_to_all | solution.py:209
  38.7 3.4 %collective-permute-start.4 = (f32[4,1]{1,0:T(4,128)S(1)}, f32[4,1]{1,0:T(4,128)S(1)}, u32[]{:S(2)}, u32[]{:S(2)}) collective-permute-start(f32[4,1]{1,0:T(4,128)S(1)} %get-tuple-element.428), channel_id=1, source_target_pairs={{0,1},{1,2},{2,3},{4,5},{5,6},{6,7},{8,9},{9,10},{10,11},{12,13},{... | collective-permute-start | bytes 56 | tf_op jit(solution)/shard_map/ppermute | solution.py:20
  47.6 4.3 %collective-permute-start.6 = (f32[4,1]{1,0:T(4,128)S(1)}, f32[4,1]{1,0:T(4,128)S(1)}, u32[]{:S(2)}, u32[]{:S(2)}) collective-permute-start(f32[4,1]{1,0:T(4,128)S(1)} %get-tuple-element.422), channel_id=1, source_target_pairs={{0,1},{1,2},{2,3},{4,5},{5,6},{6,7},{8,9},{9,10},{10,11},{12,13},{... | collective-permute-start | bytes 56 | tf_op jit(solution)/shard_map/ppermute | solution.py:20
  55.8 3.8 %collective-permute-start.8 = (f32[4,1]{1,0:T(4,128)S(1)}, f32[4,1]{1,0:T(4,128)S(1)}, u32[]{:S(2)}, u32[]{:S(2)}) collective-permute-start(f32[4,1]{1,0:T(4,128)S(1)} %get-tuple-element.416), channel_id=1, source_target_pairs={{0,1},{1,2},{2,3},{4,5},{5,6},{6,7},{8,9},{9,10},{10,11},{12,13},{... | collective-permute-start | bytes 56 | tf_op jit(solution)/shard_map/ppermute | solution.py:20
  62.7 6.0 %all-to-all-start = ((f32[8,80,4]{1,2,0:T(4,128)}), f32[8,80,4]{1,2,0:T(4,128)S(1)}, u32[]{:S(2)}, u32[]{:S(2)}) async-start(f32[8,80,4]{1,2,0:T(4,128)} %copy.28), calls=%async_computation | async-start | bytes 32768 | tf_op jit(solution)/shard_map/all_to_all | solution.py:208
  69.5 5.8 %all-to-all-done = f32[8,80,4]{1,2,0:T(4,128)S(1)} async-done(((f32[8,80,4]{1,2,0:T(4,128)}), f32[8,80,4]{1,2,0:T(4,128)S(1)}, u32[]{:S(2)}, u32[]{:S(2)}) %all-to-all-start) | async-done | bytes 10272 | tf_op jit(solution)/shard_map/all_to_all | solution.py:208
  78.7 6.5 %all-to-all-done.1 = f32[8,80,4]{1,2,0:T(4,128)S(1)} async-done(((f32[8,80,4]{1,2,0:T(4,128)}), f32[8,80,4]{1,2,0:T(4,128)S(1)}, u32[]{:S(2)}, u32[]{:S(2)}) %all-to-all-start.1) | async-done | bytes 10272 | tf_op jit(solution)/shard_map/all_to_all | solution.py:207
  86.3 3.3 %all-to-all-start.3 = ((f32[80,8,4]{0,2,1:T(4,128)}), f32[80,8,4]{0,2,1:T(4,128)S(1)}, u32[]{:S(2)}, u32[]{:S(2)}) async-start(f32[80,8,4]{0,2,1:T(4,128)} %fusion.125), calls=%async_computation.3 | async-start | bytes 32768 | tf_op jit(solution)/shard_map/all_to_all | solution.py:186
  90.2 5.9 %all-to-all-done.3 = f32[80,8,4]{0,2,1:T(4,128)S(1)} async-done(((f32[80,8,4]{0,2,1:T(4,128)}), f32[80,8,4]{0,2,1:T(4,128)S(1)}, u32[]{:S(2)}, u32[]{:S(2)}) %all-to-all-start.3) | async-done | bytes 10272 | tf_op jit(solution)/shard_map/all_to_all | solution.py:186
  99.7 6.3 %all-to-all-done.4 = f32[80,8,4]{0,2,1:T(4,128)S(1)} async-done(((f32[80,8,4]{0,2,1:T(4,128)}), f32[80,8,4]{0,2,1:T(4,128)S(1)}, u32[]{:S(2)}, u32[]{:S(2)}) %all-to-all-start.4) | async-done | bytes 10272 | tf_op jit(solution)/shard_map/all_to_all | solution.py:185
  108.7 3.8 %collective-permute-done.11 = f32[4,1]{1,0:T(4,128)S(1)} collective-permute-done((f32[4,1]{1,0:T(4,128)S(1)}, f32[4,1]{1,0:T(4,128)S(1)}, u32[]{:S(2)}, u32[]{:S(2)}) %collective-permute-start.11) | collective-permute-done | bytes 48 | tf_op jit(solution)/shard_map/ppermute | solution.py:23
  113.4 4.3 %collective-permute-start.12 = (f32[4,1]{1,0:T(4,128)S(1)}, f32[4,1]{1,0:T(4,128)S(1)}, u32[]{:S(2)}, u32[]{:S(2)}) collective-permute-start(f32[4,1]{1,0:T(4,128)S(1)} %get-tuple-element.404), channel_id=1, source_target_pairs={{0,1},{1,2},{2,3},{4,5},{5,6},{6,7},{8,9},{9,10},{10,11},{12,13},{... | collective-permute-start | bytes 56 | tf_op jit(solution)/shard_map/ppermute | solution.py:20
  121.6 3.8 %collective-permute-start.14 = (f32[4,1]{1,0:T(4,128)S(1)}, f32[4,1]{1,0:T(4,128)S(1)}, u32[]{:S(2)}, u32[]{:S(2)}) collective-permute-start(f32[4,1]{1,0:T(4,128)S(1)} %get-tuple-element.398), channel_id=1, source_target_pairs={{0,1},{1,2},{2,3},{4,5},{5,6},{6,7},{8,9},{9,10},{10,11},{12,13},{... | collective-permute-start | bytes 56 | tf_op jit(solution)/shard_map/ppermute | solution.py:20
  129.3 3.8 %collective-permute-start.16 = (f32[4,1]{1,0:T(4,128)S(1)}, f32[4,1]{1,0:T(4,128)S(1)}, u32[]{:S(2)}, u32[]{:S(2)}) collective-permute-start(f32[4,1]{1,0:T(4,128)S(1)} %get-tuple-element.392), channel_id=1, source_target_pairs={{0,1},{1,2},{2,3},{4,5},{5,6},{6,7},{8,9},{9,10},{10,11},{12,13},{... | collective-permute-start | bytes 56 | tf_op jit(solution)/shard_map/ppermute | solution.py:20
  139.3 5.6 %all-to-all-done.5 = f32[8,80,4]{1,2,0:T(4,128)S(1)} async-done(((f32[8,80,4]{1,2,0:T(4,128)}), f32[8,80,4]{1,2,0:T(4,128)S(1)}, u32[]{:S(2)}, u32[]{:S(2)}) %all-to-all-start.5) | async-done | bytes 10272 | tf_op jit(solution)/shard_map/all_to_all | solution.py:214
  145.0 3.3 %all-to-all-start.6 = ((f32[8,80,4]{1,2,0:T(4,128)}), f32[8,80,4]{1,2,0:T(4,128)S(1)}, u32[]{:S(2)}, u32[]{:S(2)}) async-start(f32[8,80,4]{1,2,0:T(4,128)} %copy.37), calls=%async_computation.6 | async-start | bytes 32768 | tf_op jit(solution)/shard_map/all_to_all | solution.py:213
  148.3 6.5 %all-to-all-done.6 = f32[8,80,4]{1,2,0:T(4,128)S(1)} async-done(((f32[8,80,4]{1,2,0:T(4,128)}), f32[8,80,4]{1,2,0:T(4,128)S(1)}, u32[]{:S(2)}, u32[]{:S(2)}) %all-to-all-start.6) | async-done | bytes 10272 | tf_op jit(solution)/shard_map/all_to_all | solution.py:213
  155.3 8.9 %all_to_all.146 = f32[80,8,4]{0,2,1:T(4,128)S(1)} all-to-all(f32[80,8,4]{0,2,1:T(4,128)S(1)} %fusion.117), channel_id=1, replica_groups=mesh['strip'=8,'cells'=4] {'strip'}, dimensions={1} | all-to-all | bytes 20480 | tf_op jit(solution)/shard_map/all_to_all | solution.py:221
  168.2 4.1 %collective-permute-done.19 = f32[1,640]{1,0:T(1,128)S(1)} collective-permute-done((f32[1,640]{1,0:T(1,128)S(1)}, f32[1,640]{1,0:T(1,128)S(1)}, u32[]{:S(2)}, u32[]{:S(2)}) %collective-permute-start.19) | collective-permute-done | bytes 2592 | tf_op jit(solution)/shard_map/ppermute | solution.py:23
  172.3 5.6 %all_gather.3 = f32[6,2560]{1,0:T(8,128)S(1)} all-gather(f32[6,640]{1,0:T(8,128)S(1)} %pad_maximum_fusion.4), channel_id=1, replica_groups=mesh['strip'=8,'cells'=4] {'cells'}, dimensions={1}, use_global_device_ids=true | all-gather | bytes 76800 | tf_op jit(solution)/shard_map/all_gather | solution.py:227
  178.2 4.1 %while.27 = (s32[]{:T(128)}, f32[2,2,2048]{2,1,0:T(2,128)S(1)}, s32[2,2048]{1,0:T(2,128)S(1)}, bf16[2,2048]{1,0:T(2,128)(2,1)S(1)}, bf16[2,2048]{1,0:T(2,128)(2,...) while((s32[]{:T(128)}, f32[2,2,2048]{2,1,0:T(2,128)S(1)}, ...), condition=%wide.region_6.7_spmd, body=%wide.region_3.6_spmd.sunk | while | flops 174956544 | bytes 13811829 | solution.py:172
  (203 shorter events, 62.5 us)
Async XLA Ops:
  22.6 15.2 %collective-permute-start = (f32[1,640]{1,0:T(1,128)S(1)}, f32[1,640]{1,0:T(1,128)S(1)}, u32[]{:S(2)}, u32[]{:S(2)}) collective-permute-start(f32[1,640]{1,0:T(1,128)S(1)} %get-tuple-element.440), channel_id=1, source_target_pairs={{0,4},{4,8},{8,12},{12,16},{16,20},{20,24},{24,28},{1,5},{5,9},{9,... | collective-permute-start | bytes 7688 | tf_op jit(solution)/shard_map/ppermute | solution.py:20
  26.0 11.8 %collective-permute-start.1 = (f32[1,640]{1,0:T(1,128)S(1)}, f32[1,640]{1,0:T(1,128)S(1)}, u32[]{:S(2)}, u32[]{:S(2)}) collective-permute-start(f32[1,640]{1,0:T(1,128)S(1)} %get-tuple-element.439), channel_id=1, source_target_pairs={{4,0},{8,4},{12,8},{16,12},{20,16},{24,20},{28,24},{5,1},{9,5},{13... | collective-permute-start | bytes 7688 | tf_op jit(solution)/shard_map/ppermute | solution.py:23
  27.4 10.3 %collective-permute-start.2 = (f32[4,1]{1,0:T(4,128)S(1)}, f32[4,1]{1,0:T(4,128)S(1)}, u32[]{:S(2)}, u32[]{:S(2)}) collective-permute-start(f32[4,1]{1,0:T(4,128)S(1)} %get-tuple-element.434), channel_id=1, source_target_pairs={{0,1},{1,2},{2,3},{4,5},{5,6},{6,7},{8,9},{9,10},{10,11},{12,13},{... | collective-permute-start | bytes 56 | tf_op jit(solution)/shard_map/ppermute | solution.py:20
  28.7 9.0 %collective-permute-start.3 = (f32[4,1]{1,0:T(4,128)S(1)}, f32[4,1]{1,0:T(4,128)S(1)}, u32[]{:S(2)}, u32[]{:S(2)}) collective-permute-start(f32[4,1]{1,0:T(4,128)S(1)} %get-tuple-element.433), channel_id=1, source_target_pairs={{1,0},{2,1},{3,2},{5,4},{6,5},{7,6},{9,8},{10,9},{11,10},{13,12},{... | collective-permute-start | bytes 56 | tf_op jit(solution)/shard_map/ppermute | solution.py:23
  30.7 32.0 %all-to-all-start.2 = ((f32[8,80,4]{1,2,0:T(4,128)}), f32[8,80,4]{1,2,0:T(4,128)S(1)}, u32[]{:S(2)}, u32[]{:S(2)}) async-start(f32[8,80,4]{1,2,0:T(4,128)} %copy.30), calls=%async_computation.2 | async-start | bytes 32768 | tf_op jit(solution)/shard_map/all_to_all | solution.py:209
  38.7 4.8 %collective-permute-start.4 = (f32[4,1]{1,0:T(4,128)S(1)}, f32[4,1]{1,0:T(4,128)S(1)}, u32[]{:S(2)}, u32[]{:S(2)}) collective-permute-start(f32[4,1]{1,0:T(4,128)S(1)} %get-tuple-element.428), channel_id=1, source_target_pairs={{0,1},{1,2},{2,3},{4,5},{5,6},{6,7},{8,9},{9,10},{10,11},{12,13},{... | collective-permute-start | bytes 56 | tf_op jit(solution)/shard_map/ppermute | solution.py:20
  42.1 4.6 %collective-permute-start.5 = (f32[4,1]{1,0:T(4,128)S(1)}, f32[4,1]{1,0:T(4,128)S(1)}, u32[]{:S(2)}, u32[]{:S(2)}) collective-permute-start(f32[4,1]{1,0:T(4,128)S(1)} %get-tuple-element.427), channel_id=1, source_target_pairs={{1,0},{2,1},{3,2},{5,4},{6,5},{7,6},{9,8},{10,9},{11,10},{13,12},{... | collective-permute-start | bytes 56 | tf_op jit(solution)/shard_map/ppermute | solution.py:23
  47.6 5.6 %collective-permute-start.6 = (f32[4,1]{1,0:T(4,128)S(1)}, f32[4,1]{1,0:T(4,128)S(1)}, u32[]{:S(2)}, u32[]{:S(2)}) collective-permute-start(f32[4,1]{1,0:T(4,128)S(1)} %get-tuple-element.422), channel_id=1, source_target_pairs={{0,1},{1,2},{2,3},{4,5},{5,6},{6,7},{8,9},{9,10},{10,11},{12,13},{... | collective-permute-start | bytes 56 | tf_op jit(solution)/shard_map/ppermute | solution.py:20
  51.9 3.1 %collective-permute-start.7 = (f32[4,1]{1,0:T(4,128)S(1)}, f32[4,1]{1,0:T(4,128)S(1)}, u32[]{:S(2)}, u32[]{:S(2)}) collective-permute-start(f32[4,1]{1,0:T(4,128)S(1)} %get-tuple-element.421), channel_id=1, source_target_pairs={{1,0},{2,1},{3,2},{5,4},{6,5},{7,6},{9,8},{10,9},{11,10},{13,12},{... | collective-permute-start | bytes 56 | tf_op jit(solution)/shard_map/ppermute | solution.py:23
  55.8 5.8 %collective-permute-start.8 = (f32[4,1]{1,0:T(4,128)S(1)}, f32[4,1]{1,0:T(4,128)S(1)}, u32[]{:S(2)}, u32[]{:S(2)}) collective-permute-start(f32[4,1]{1,0:T(4,128)S(1)} %get-tuple-element.416), channel_id=1, source_target_pairs={{0,1},{1,2},{2,3},{4,5},{5,6},{6,7},{8,9},{9,10},{10,11},{12,13},{... | collective-permute-start | bytes 56 | tf_op jit(solution)/shard_map/ppermute | solution.py:20
  62.7 12.6 %all-to-all-start = ((f32[8,80,4]{1,2,0:T(4,128)}), f32[8,80,4]{1,2,0:T(4,128)S(1)}, u32[]{:S(2)}, u32[]{:S(2)}) async-start(f32[8,80,4]{1,2,0:T(4,128)} %copy.28), calls=%async_computation | async-start | bytes 32768 | tf_op jit(solution)/shard_map/all_to_all | solution.py:208
  75.3 9.8 %all-to-all-start.1 = ((f32[8,80,4]{1,2,0:T(4,128)}), f32[8,80,4]{1,2,0:T(4,128)S(1)}, u32[]{:S(2)}, u32[]{:S(2)}) async-start(f32[8,80,4]{1,2,0:T(4,128)} %copy.29), calls=%async_computation.1 | async-start | bytes 32768 | tf_op jit(solution)/shard_map/all_to_all | solution.py:207
  86.3 9.9 %all-to-all-start.3 = ((f32[80,8,4]{0,2,1:T(4,128)}), f32[80,8,4]{0,2,1:T(4,128)S(1)}, u32[]{:S(2)}, u32[]{:S(2)}) async-start(f32[80,8,4]{0,2,1:T(4,128)} %fusion.125), calls=%async_computation.3 | async-start | bytes 32768 | tf_op jit(solution)/shard_map/all_to_all | solution.py:186
  96.1 9.8 %all-to-all-start.4 = ((f32[80,8,4]{0,2,1:T(4,128)}), f32[80,8,4]{0,2,1:T(4,128)S(1)}, u32[]{:S(2)}, u32[]{:S(2)}) async-start(f32[80,8,4]{0,2,1:T(4,128)} %bitcast.42), calls=%async_computation.4 | async-start | bytes 32768 | tf_op jit(solution)/shard_map/all_to_all | solution.py:185
  107.4 5.1 %collective-permute-start.11 = (f32[4,1]{1,0:T(4,128)S(1)}, f32[4,1]{1,0:T(4,128)S(1)}, u32[]{:S(2)}, u32[]{:S(2)}) collective-permute-start(f32[4,1]{1,0:T(4,128)S(1)} %get-tuple-element.409), channel_id=1, source_target_pairs={{1,0},{2,1},{3,2},{5,4},{6,5},{7,6},{9,8},{10,9},{11,10},{13,12},{... | collective-permute-start | bytes 56 | tf_op jit(solution)/shard_map/ppermute | solution.py:23
  113.4 5.6 %collective-permute-start.12 = (f32[4,1]{1,0:T(4,128)S(1)}, f32[4,1]{1,0:T(4,128)S(1)}, u32[]{:S(2)}, u32[]{:S(2)}) collective-permute-start(f32[4,1]{1,0:T(4,128)S(1)} %get-tuple-element.404), channel_id=1, source_target_pairs={{0,1},{1,2},{2,3},{4,5},{5,6},{6,7},{8,9},{9,10},{10,11},{12,13},{... | collective-permute-start | bytes 56 | tf_op jit(solution)/shard_map/ppermute | solution.py:20
  121.6 5.1 %collective-permute-start.14 = (f32[4,1]{1,0:T(4,128)S(1)}, f32[4,1]{1,0:T(4,128)S(1)}, u32[]{:S(2)}, u32[]{:S(2)}) collective-permute-start(f32[4,1]{1,0:T(4,128)S(1)} %get-tuple-element.398), channel_id=1, source_target_pairs={{0,1},{1,2},{2,3},{4,5},{5,6},{6,7},{8,9},{9,10},{10,11},{12,13},{... | collective-permute-start | bytes 56 | tf_op jit(solution)/shard_map/ppermute | solution.py:20
  125.4 3.1 %collective-permute-start.15 = (f32[4,1]{1,0:T(4,128)S(1)}, f32[4,1]{1,0:T(4,128)S(1)}, u32[]{:S(2)}, u32[]{:S(2)}) collective-permute-start(f32[4,1]{1,0:T(4,128)S(1)} %get-tuple-element.397), channel_id=1, source_target_pairs={{1,0},{2,1},{3,2},{5,4},{6,5},{7,6},{9,8},{10,9},{11,10},{13,12},{... | collective-permute-start | bytes 56 | tf_op jit(solution)/shard_map/ppermute | solution.py:23
  129.3 9.2 %collective-permute-start.16 = (f32[4,1]{1,0:T(4,128)S(1)}, f32[4,1]{1,0:T(4,128)S(1)}, u32[]{:S(2)}, u32[]{:S(2)}) collective-permute-start(f32[4,1]{1,0:T(4,128)S(1)} %get-tuple-element.392), channel_id=1, source_target_pairs={{0,1},{1,2},{2,3},{4,5},{5,6},{6,7},{8,9},{9,10},{10,11},{12,13},{... | collective-permute-start | bytes 56 | tf_op jit(solution)/shard_map/ppermute | solution.py:20
  133.1 5.3 %collective-permute-start.17 = (f32[4,1]{1,0:T(4,128)S(1)}, f32[4,1]{1,0:T(4,128)S(1)}, u32[]{:S(2)}, u32[]{:S(2)}) collective-permute-start(f32[4,1]{1,0:T(4,128)S(1)} %get-tuple-element.391), channel_id=1, source_target_pairs={{1,0},{2,1},{3,2},{5,4},{6,5},{7,6},{9,8},{10,9},{11,10},{13,12},{... | collective-permute-start | bytes 56 | tf_op jit(solution)/shard_map/ppermute | solution.py:23
  135.1 9.8 %all-to-all-start.5 = ((f32[8,80,4]{1,2,0:T(4,128)}), f32[8,80,4]{1,2,0:T(4,128)S(1)}, u32[]{:S(2)}, u32[]{:S(2)}) async-start(f32[8,80,4]{1,2,0:T(4,128)} %copy.36), calls=%async_computation.5 | async-start | bytes 32768 | tf_op jit(solution)/shard_map/all_to_all | solution.py:214
  145.0 9.9 %all-to-all-start.6 = ((f32[8,80,4]{1,2,0:T(4,128)}), f32[8,80,4]{1,2,0:T(4,128)S(1)}, u32[]{:S(2)}, u32[]{:S(2)}) async-start(f32[8,80,4]{1,2,0:T(4,128)} %copy.37), calls=%async_computation.6 | async-start | bytes 32768 | tf_op jit(solution)/shard_map/all_to_all | solution.py:213
  164.4 3.8 %collective-permute-start.18 = (f32[1,640]{1,0:T(1,128)S(1)}, f32[1,640]{1,0:T(1,128)S(1)}, u32[]{:S(2)}, u32[]{:S(2)}) collective-permute-start(f32[1,640]{1,0:T(1,128)S(1)} %get-tuple-element.385), channel_id=1, source_target_pairs={{0,4},{4,8},{8,12},{12,16},{16,20},{20,24},{24,28},{1,5},{5,9},{9,... | collective-permute-start | bytes 7688 | tf_op jit(solution)/shard_map/ppermute | solution.py:20
  166.8 5.5 %collective-permute-start.19 = (f32[1,640]{1,0:T(1,128)S(1)}, f32[1,640]{1,0:T(1,128)S(1)}, u32[]{:S(2)}, u32[]{:S(2)}) collective-permute-start(f32[1,640]{1,0:T(1,128)S(1)} %get-tuple-element.386), channel_id=1, source_target_pairs={{4,0},{8,4},{12,8},{16,12},{20,16},{24,20},{28,24},{5,1},{9,5},{13... | collective-permute-start | bytes 7688 | tf_op jit(solution)/shard_map/ppermute | solution.py:23
  (9 other events, 172.0 us)
where the time goes:
time: 185 us; the launch traced here: 183 us
  starting transfers between devices  74.3 us (40%)
  waiting for transfers between devices  54.1 us (29%)
  blocking collectives  27.7 us (15%)
  local copies, waits for them, and re-layouts  9.19 us (5%)
  other arithmetic  8.85 us (5%)
  matrix products  6.98 us (4%)
    ppermute x10, starting transfers between devices, padded_2(): lax.ppermute(lax.slice_in_dim(block, block.shape[dim] - width, None, axis...  31.8 us
    ppermute x10, waiting for transfers between devices, padded_2(): lax.ppermute(lax.slice_in_dim(block, 0, width, axis=dim), axis, backward)  17.5 us
    psum x1, blocking collectives, local(): whole = lax.psum(partial_value, 'cells')  13.2 us
    all_to_all x2, waiting for transfers between devices, local(): lax.all_to_all(middle.T, 'strip', split_axis=0, concat_axis=1, tiled=True)  13 us
    ppermute x10, starting transfers between devices, padded_2(): lax.ppermute(lax.slice_in_dim(block, 0, width, axis=dim), axis, backward)  12.9 us
    all_to_all x2, waiting for transfers between devices, local(): lax.all_to_all(current.T, 'strip', split_axis=0, concat_axis=1, tiled=True)  11.4 us
    all_to_all x2, starting transfers between devices, local(): lax.all_to_all(current.T, 'strip', split_axis=0, concat_axis=1, tiled=True)  9.32 us
    all_to_all x1, blocking collectives, local(): lax.all_to_all(current_col, 'strip', split_axis=1, concat_axis=0, tiled=T...  8.94 us
  transfers between devices with their start and end apart: 27, of which 13 were waited for; matrix products, arithmetic and copies ran while one was open for 4% of the time, Pallas kernels for 0%

commit v1 on v0

v1 whole, which is shorter than its diff:
```python
import functools

import jax
import jax.numpy as jnp
from jax import lax
from jax.experimental import pallas as pl
from jax.experimental.pallas import tpu as pltpu
from jax.sharding import PartitionSpec as P

SWEEPS = 3
STEPS = 2
LANES = 128
GROUP = 8

coupling = 2.0
floor_level = 0.5
block_low = -0.002
block_span = 0.152
code_top = 65535.0
code_half = 32768.0

f32 = jnp.float32
bf16 = jnp.bfloat16


def iota(shape, axis):
    return lax.broadcasted_iota(jnp.int32, shape, axis)


def halves(values):
    high = values.astype(bf16)
    return high, (values - high.astype(f32)).astype(bf16)


def last_dims(left, right):
    return lax.dot_general(left, right, (((1,), (1,)), ((), ())), preferred_element_type=f32)


def pick(index, first, near, far):
    return jnp.where(index == first, near, jnp.where(index == first + 1, far, 0.0))


def rounded(values):
    return values.astype(bf16).astype(f32)


def splat_kernel(tiles, parts, rows_ref, cols_ref, fracs_ref, pin_weights_ref, cap_ref, block_ref, out_ref):
    depth = cap_ref.shape[0]
    height = parts * depth
    rows, cols, sizes = rows_ref[...], cols_ref[...], pin_weights_ref[...]
    place = iota((height * (tiles + 1), LANES), 0)
    group, inner = place // height, place % height
    keys = ((inner // depth) * tiles + group - 1) * depth + inner % depth
    lane = iota((LANES + 8, LANES), 0)
    tables, lanes = [], []
    for j in range(rows.shape[0]):
        fy, fx = fracs_ref[0, j : j + 1, :], fracs_ref[1, j : j + 1, :]
        size, col = sizes[j : j + 1], cols[j : j + 1]
        key = (col >> 7) * depth + rows[j : j + 1]
        tables.append(pick(keys, key, rounded(size * (1.0 - fy)), rounded(size * fy)).astype(bf16))
        lanes.append(pick(lane, col & 127, rounded(1.0 - fx), rounded(fx)).astype(bf16))
    total = last_dims(jnp.concatenate(tables, 1), jnp.concatenate(lanes, 1))
    first_lane = iota((height, LANES), 1) == 0
    for t in range(tiles):
        own = total[(t + 1) * height : (t + 2) * height, :LANES]
        spill = total[t * height : (t + 1) * height, LANES : LANES + 1]
        own = own + jnp.where(first_lane, spill, 0.0)
        out_ref[:height, t * LANES : (t + 1) * LANES] = own.astype(bf16)
    weights = cap_ref[...].astype(f32) * (1.0 - block_ref[...])
    high, low = halves(weights)
    rest = jnp.zeros((height - 2 * depth, weights.shape[1]), f32)
    out_ref[height:, :] = jnp.concatenate([high.astype(f32), low.astype(f32), rest], 0).astype(bf16)


def along_lines(values):
    width = values.shape[1]
    column = iota(values.shape, 1)
    left = jnp.where(column == 0, values, pltpu.roll(values, 1, 1))
    right = jnp.where(column == width - 1, values, pltpu.roll(values, width - 1, 1))
    return 2.0 * values - left - right


def across_lines(values):
    height = values.shape[0]
    row = iota(values.shape, 0)
    above = jnp.where(row == 0, values, pltpu.roll(values, 1, 0))
    below = jnp.where(row == height - 1, values, pltpu.roll(values, height - 1, 0))
    return 2.0 * values - above - below


def row_blockwise(residual, pairs_ref):
    high, low = halves(residual)
    result = []
    for k in range(pairs_ref.shape[0]):
        cut = slice(k * LANES, (k + 1) * LANES)
        pair = pairs_ref[k]
        both = last_dims(jnp.concatenate([high[:, cut], low[:, cut]], 1), jnp.concatenate([pair, pair], 1))
        result.append(both[:, :LANES] + both[:, LANES:])
    return jnp.concatenate(result, 1)


def col_blockwise(residual, blocks):
    high, low = halves(residual)
    count, size = len(blocks), blocks[0][0].shape[0]
    result = []
    for k, (block_high, block_low_part) in enumerate(blocks):
        cut = slice(k * size, (k + 1) * size)
        dot = functools.partial(jnp.dot, preferred_element_type=f32)
        result.append(dot(block_high, high[cut]) + (dot(block_low_part, high[cut]) + dot(block_high, low[cut])))
    return result[0] if count == 1 else jnp.concatenate(result, 0)


def each(count, body):
    if count == 1:
        body(0)
    else:
        pl.loop(0, count)(body)


def field_kernel(
    sizes, spot_ref, sent_ref, codes_ref, col_blocks_ref, rows_ref, cols_ref, fracs_ref,
    final_ref, velocity_ref, pairs, weights_ref, source_ref, field_ref,
):
    depth, tiles, parts, strips = sizes
    width_part = tiles * LANES
    width = parts * width_part
    height = strips * depth
    chunk = min(GROUP, strips) * depth
    chunks = height // chunk
    strip, part = spot_ref[0], spot_ref[1]

    def unpack(k):
        code = codes_ref[pl.ds(pl.multiple_of(k * LANES, LANES), LANES), :].astype(f32)
        high, low = halves((code + code_half) * (block_span / code_top) + block_low)
        pairs[k, :LANES, :] = high
        pairs[k, LANES:, :] = low

    for k in range(pairs.shape[0]):
        unpack(k)

    sent_rows = 2 * parts * depth
    span = chunk // depth * parts * sent_rows
    target, origin = iota((parts * chunk, span), 0), iota((parts * chunk, span), 1)
    device, slot = origin // sent_rows, origin % sent_rows
    row_here = target % chunk - (device // parts) * depth
    side = target // chunk
    first = parts * depth
    terms = (slot < first) & (slot // depth == side) & (slot % depth == row_here)
    pieces = (slot >= first) & (slot < first + 2 * depth) & (device % parts == side) & (slot % depth == row_here)
    chosen = jnp.concatenate([jnp.where(terms, 1.0, 0.0), jnp.where(pieces, 1.0, 0.0)], 0).astype(bf16)

    @functools.partial(each, chunks)
    def place(g):
        got = jnp.dot(
            chosen, sent_ref[pl.ds(pl.multiple_of(g * span, span), span), :], preferred_element_type=f32
        )
        here = pl.ds(pl.multiple_of(g * chunk, chunk), chunk)
        for p in range(parts):
            cut = slice(p * width_part, (p + 1) * width_part)
            weight = got[(parts + p) * chunk : (parts + p + 1) * chunk]
            weights_ref[here, cut] = weight
            source_ref[here, cut] = got[p * chunk : (p + 1) * chunk] / weight

    lanes_at_once = width if chunks == 1 else LANES
    col_blocks = [halves(col_blocks_ref[k]) for k in range(col_blocks_ref.shape[0])]
    inner = pl.ds(8, height)

    @functools.partial(each, width // lanes_at_once)
    def start(t):
        cut = pl.ds(pl.multiple_of(t * lanes_at_once, lanes_at_once), lanes_at_once)
        current = source_ref[:, cut]
        field_ref[inner, cut] = current
        source_ref[:, cut] = weights_ref[:, cut] * current - coupling * across_lines(current)

    for step in range(STEPS):

        @functools.partial(each, chunks)
        def solve_rows(g):
            here = pl.ds(pl.multiple_of(g * chunk, chunk), chunk)
            there = pl.ds(pl.multiple_of(g * chunk + 8, 8), chunk)
            source, weights, current = source_ref[here, :], weights_ref[here, :], field_ref[there, :]
            for sweep in range(SWEEPS):
                residual = source - (weights * current + coupling * along_lines(current))
                current = current + row_blockwise(residual, pairs)
            field_ref[there, :] = current
            source_ref[here, :] = weights * current - coupling * along_lines(current)

        @functools.partial(each, width // lanes_at_once)
        def solve_cols(t):
            cut = pl.ds(pl.multiple_of(t * lanes_at_once, lanes_at_once), lanes_at_once)
            middle, weights, current = source_ref[:, cut], weights_ref[:, cut], field_ref[inner, cut]
            for sweep in range(SWEEPS):
                residual = middle - (weights * current + coupling * across_lines(current))
                current = current + col_blockwise(residual, col_blocks)
            field_ref[inner, cut] = current
            if step + 1 < STEPS:
                source_ref[:, cut] = weights * current - coupling * across_lines(current)
            else:
                field_ref[:8, cut] = jnp.broadcast_to(current[:1], (8, lanes_at_once))
                field_ref[height + 8 :, cut] = jnp.broadcast_to(current[-1:], (8, lanes_at_once))

    row0 = strip * depth
    columns = pl.ds(pl.multiple_of(part * width_part, LANES), width_part)
    base, shift = pl.multiple_of(row0 // 8 * 8, 8), 17 - row0 % 8
    final_ref[...] = pltpu.roll(field_ref[pl.ds(base, 24), columns], shift, 0)[1 : 1 + depth]

    window = pltpu.roll(field_ref[pl.ds(base, 24), :], shift, 0)
    above, centre, below = window[:8], pltpu.roll(window, 23, 0)[:8], pltpu.roll(window, 22, 0)[:8]
    column = iota(centre.shape, 1)
    left = jnp.where(column == 0, centre, pltpu.roll(centre, 1, 1))
    right = jnp.where(column == width - 1, centre, pltpu.roll(centre, width - 1, 1))
    scale = jnp.maximum(centre, floor_level)
    velocity_y = rounded(-(0.5 * (below - above)) / scale)
    velocity_x = rounded(-(0.5 * (right - left)) / scale)

    upper = iota((8, LANES), 0) < depth

    def stacked(values):
        stack = []
        for t in range(0, parts * tiles, 2):
            even = values[:, t * LANES : (t + 1) * LANES]
            odd = values[:, (t + 1) * LANES : (t + 2) * LANES]
            stack.append(jnp.where(upper, even, pltpu.roll(odd, depth, 0)))
        return jnp.concatenate(stack, 0)

    stack_y, stack_x = stacked(velocity_y), stacked(velocity_x)
    many = stack_y.shape[0]
    next_y = pltpu.roll(stack_y, many - depth, 0)
    next_x = pltpu.roll(stack_x, many - depth, 0)
    turned = [stack_y.T, next_y.T[:8], stack_x.T, next_x.T[:8]]
    table = jnp.concatenate(turned, 0).astype(bf16)
    rows, cols = rows_ref[...], cols_ref[...]
    keys, lane = iota((many, LANES), 0), iota((LANES + 8, LANES), 0)
    for j in range(rows.shape[0]):
        fy, fx = fracs_ref[0, j : j + 1, :], fracs_ref[1, j : j + 1, :]
        col = cols[j : j + 1]
        key = (col >> 7) * depth + rows[j : j + 1]
        look = pick(keys, key, rounded(1.0 - fy), rounded(fy)).astype(bf16)
        sampled = jnp.dot(table, look, preferred_element_type=f32)
        share = pick(lane, col & 127, rounded(1.0 - fx), rounded(fx))
        cut = slice(j * LANES, (j + 1) * LANES)
        velocity_ref[0:1, cut] = jnp.sum(sampled[: LANES + 8] * share, 0, keepdims=True)
        velocity_ref[1:2, cut] = jnp.sum(sampled[LANES + 8 :] * share, 0, keepdims=True)


def local(pin_rows, pin_cols, pin_fracs, pin_weights, capacity, blockage, row_blocks, col_blocks):
    depth, width_part = capacity.shape
    parts, strips = lax.axis_size("cells"), lax.axis_size("strip")
    tiles = width_part // LANES
    height, width = depth * strips, width_part * parts
    pins = pin_rows.shape[0]
    by_lane = (pins // LANES, LANES)
    rows, cols = pin_rows.reshape(by_lane), pin_cols.reshape(by_lane)
    fracs, sizes = pin_fracs.reshape((2,) + by_lane), pin_weights.reshape(by_lane)
    vmem = pl.BlockSpec(memory_space=pltpu.VMEM)
    params = pltpu.CompilerParams(vmem_limit_bytes=60 * 1024 * 1024)

    codes = jnp.round((row_blocks - block_low) * (code_top / block_span))
    codes = (jnp.clip(codes, 0.0, code_top) - code_half).astype(jnp.int16).reshape(-1, LANES)
    codes = lax.all_gather(codes, "cells", axis=0, tiled=True)

    message = pl.pallas_call(
        functools.partial(splat_kernel, tiles, parts),
        out_shape=jax.ShapeDtypeStruct((2 * parts * depth, width_part), bf16),
        in_specs=[vmem] * 6,
        out_specs=vmem,
        compiler_params=params,
        name="splat",
    )(rows, cols, fracs, sizes, capacity, blockage)
    sent = lax.all_gather(message, ("strip", "cells"), axis=0, tiled=True)

    spot = jnp.stack([lax.axis_index("strip"), lax.axis_index("cells")]).astype(jnp.int32)
    final, velocity = pl.pallas_call(
        functools.partial(field_kernel, (depth, tiles, parts, strips)),
        out_shape=(
            jax.ShapeDtypeStruct((depth, width_part), f32),
            jax.ShapeDtypeStruct((2, pins), f32),
        ),
        in_specs=[pl.BlockSpec(memory_space=pltpu.SMEM)] + [vmem] * 6,
        out_specs=(vmem, vmem),
        scratch_shapes=[
            pltpu.VMEM((width // LANES, 2 * LANES, LANES), bf16),
            pltpu.VMEM((height, width), f32),
            pltpu.VMEM((height, width), f32),
            pltpu.VMEM((height + 16, width), f32),
        ],
        compiler_params=params,
        name="field",
    )(spot, sent, codes, col_blocks, rows, cols, fracs)
    return final, velocity


def solution(mesh):
    placed = (
        P(("strip", "cells")),
        P(("strip", "cells")),
        P(None, ("strip", "cells")),
        P(("strip", "cells")),
        P("strip", "cells"),
        P("strip", "cells"),
        P("cells", None, None),
        P(),
    )
    return jax.shard_map(
        local,
        mesh=mesh,
        in_specs=placed,
        out_specs=(P("strip", "cells"), P(None, ("strip", "cells"))),
        check_vma=False,
    )
```

time: 185 us -> 86.4 us (0.47)
  starting transfers between devices: 74.3 us -> 0.04 us
  blocking collectives: 27.7 us -> 9.81 us
  Pallas kernels: 0 us -> 13.4 us
  between operations: 1.26 us -> 14 us
  waiting for transfers between devices: 54.1 us -> 45.7 us
  local copies, waits for them, and re-layouts: 9.19 us -> 1.37 us
  other arithmetic: 8.85 us -> 1.68 us
  matrix products: 6.98 us -> 0 us
    all_gather x0 -> x1, waiting for transfers between devices: none -> 45.7 us  [local(): sent = lax.all_gather(message, ('strip', 'cells'), axis=0, tiled=True)]
    ppermute x20 -> x0, starting transfers between devices: 44.7 us -> none  [the longest x10 31.8 us: padded_2(): lax.ppermute(lax.slice_in_dim(block, block.shape[dim] - width, None, axis...]
    all_to_all x7 -> x0, waiting for transfers between devices: 36.6 us -> none  [the longest x2 13 us: local(): lax.all_to_all(middle.T, 'strip', split_axis=0, concat_axis=1, tiled=True)]
    all_to_all x7 -> x0, starting transfers between devices: 29.6 us -> none  [the longest x2 9.32 us: local(): lax.all_to_all(current.T, 'strip', split_axis=0, concat_axis=1, tiled=True)]
    ppermute x20 -> x0, waiting for transfers between devices: 17.5 us -> none  [the longest x10 17.5 us: padded_2(): lax.ppermute(lax.slice_in_dim(block, 0, width, axis=dim), axis, backward)]
    pallas_call x0 -> x2, Pallas kernels: none -> 13.4 us  [the longest x1 11 us: local(): pl.pallas_call(functools.partial(field_kernel, (depth, tiles, parts, stri...]
    psum x1 -> x0, blocking collectives: 13.2 us -> none  [local(): whole = lax.psum(partial_value, 'cells')]
    all_to_all x1 -> x0, blocking collectives: 8.94 us -> none  [local(): lax.all_to_all(current_col, 'strip', split_axis=1, concat_axis=0, tiled=T...]
  transfers between devices with their start and end apart: 27 -> 1, of which waited for: 13 -> 1; matrix products, arithmetic and copies ran while one was open for 4% -> 2% of each run, Pallas kernels for 0% -> 0%
where the time goes in v1:
time: 86.4 us; the launch traced here: 86.1 us
  waiting for transfers between devices  45.7 us (53%)
  between operations  14 us (16%)
  Pallas kernels  13.4 us (16%)
  blocking collectives  9.81 us (11%)
  other arithmetic  1.68 us (2%)
  local copies, waits for them, and re-layouts  1.37 us (2%)
    all_gather x1, waiting for transfers between devices, local(): sent = lax.all_gather(message, ('strip', 'cells'), axis=0, tiled=True)  45.7 us
    pallas_call x1, Pallas kernels, local(): pl.pallas_call(functools.partial(field_kernel, (depth, tiles, parts, stri...  11 us
    all_gather x1, blocking collectives, local(): codes = lax.all_gather(codes, 'cells', axis=0, tiled=True)  9.81 us
    pallas_call x1, Pallas kernels, local(): pl.pallas_call(functools.partial(splat_kernel, tiles, parts), out_shape=j...  2.41 us
  transfers between devices with their start and end apart: 1, of which 1 were waited for; matrix products, arithmetic and copies ran while one was open for 2% of the time, Pallas kernels for 0%

profile of v1, /device:TPU:0, one launch (start us, length us, event | category | flops | bytes accessed | tf_op | source)
XLA Modules:
  0.0 86.1 jit_solution(10563297646129557788)
XLA Ops:
  7.2 0.0 all-gather.2.cloned.1.call-start
  7.2 1.4 %copy.12 = f32[1,2,32,128]{3,2,1,0:T(8,128)} copy(f32[1,2,32,128]{3,1,2,0:T(2,128)} %bitcast.17) | data formatting | bytes 65536
  8.6 2.4 %splat.1 = bf16[32,640]{1,0:T(8,128)(2,1)} custom-call(s32[32,128]{1,0:T(8,128)} %bitcast.13, s32[32,128]{1,0:T(8,128)} %bitcast.15, f32[2,32,128]{2,1,0:T(8,128)} %bitcast.11, f32[32,128]{1,0:T(8,128)} %bitcast.18, s32[4,640]{1,0:T(4,128)} %cap_ref.1, f32[4,640]{1,0:T(4,128)} %block_ref.1), custom_call_target="tpu_custom_call" | custom-call | tf_op jit(solution)/shard_map/splat/pallas_call | solution.py:262
  11.0 0.0 all-gather.2.cloned.1.call-update
  11.0 0.6 pad_add_fusion.spot_ref
  11.6 1.1 %add_convert_fusion = s16[5,128,128]{2,1,0:T(8,128)(2,1)S(1)} fusion(f32[5,128,128]{2,1,0:T(8,128)} %param.14), kind=kLoop, calls=%fused_computation | loop fusion | flops 491520 | bytes 491520 | tf_op jit(solution)/shard_map/convert_element_type | solution.py:259
  12.7 9.8 %all_gather.7.codes_ref = s16[2560,128]{1,0:T(8,128)(2,1)} all-gather(s16[640,128]{1,0:T(8,128)(2,1)S(1)} %bitcast.10), channel_id=1, replica_groups=mesh['strip'=8,'cells'=4] {'cells'}, dimensions={0}, use_global_device_ids=true | all-gather | bytes 819200 | tf_op jit(solution)/shard_map/all_gather | solution.py:260
  22.5 45.7 %all-gather.2.cloned.1.call-done.sent_ref = bf16[1024,640]{1,0:T(8,128)(2,1)} async-done(((bf16[32,640]{1,0:T(8,128)(2,1)}), bf16[1024,640]{1,0:T(8,128)(2,1)}) %all-gather.2.cloned.1.call-update) | async-done | bytes 1310736 | tf_op jit(solution)/shard_map/all_gather | solution.py:270
  68.2 11.0 %field.1 = (f32[4,640]{1,0:T(4,128)}, f32[2,4096]{1,0:T(2,128)}) custom-call(s32[2]{0:T(128)} %pad_add_fusion.spot_ref, bf16[1024,640]{1,0:T(8,128)(2,1)} %all-gather.2.cloned.1.call-done.sent_ref, s16[2560,128]{1,0:T(8,128)(2,1)} %all_gather.7.codes_ref, f32[1,32,32]{2,1,0:T(8,128)} %col_blocks_ref.1, s32[32,128]{1,0:T(8,128)} %bitcast.14, ...), custom_call_target="tpu_custom_call" | custom-call | tf_op jit(solution)/shard_map/field/pallas_call | solution.py:273
Async XLA Ops:
  7.2 61.0 %all-gather.2.cloned.1.call-start = ((), (), s32[]{:S(2)}) async-start(), calls=%async_computation | async-start | bytes 1351680 | tf_op jit(solution)/shard_map/all_gather | solution.py:270
Sparse Core Ops, SparseCore 0:
  11.1 57.0 all-gather.1

commit v2 on v1

--- a/solution.py
+++ b/solution.py
@@ -14,10 +14,11 @@
 
 coupling = 2.0
 floor_level = 0.5
-block_low = -0.002
-block_span = 0.152
+weight_low, weight_span = 0.5, 3.5
+term_low, term_octaves = -20.0, 34.0
 code_top = 65535.0
 code_half = 32768.0
+log_two = 0.6931471805599453
 
 f32 = jnp.float32
 bf16 = jnp.bfloat16
@@ -44,7 +45,28 @@
     return values.astype(bf16).astype(f32)
 
 
-def splat_kernel(tiles, parts, rows_ref, cols_ref, fracs_ref, pin_weights_ref, cap_ref, block_ref, out_ref):
+def coded(share):
+    return jnp.clip(jnp.round(share * code_top), 0.0, code_top) - code_half
+
+
+def stored(codes):
+    return codes.astype(jnp.int32).astype(jnp.int16)
+
+
+def density_codes(values):
+    octave = jnp.log(jnp.maximum(values, 2.0**-40)) * (1.0 / log_two)
+    return stored(coded((octave - term_low) * (1.0 / term_octaves)))
+
+
+def densities(codes):
+    codes = codes.astype(f32)
+    octave = (codes + code_half) * (term_octaves / code_top) + term_low
+    return jnp.where(codes == -code_half, 0.0, jnp.exp(octave * log_two))
+
+
+def splat_kernel(
+    tiles, parts, rows_ref, cols_ref, fracs_ref, pin_weights_ref, cap_ref, block_ref, out_ref
+):
     depth = cap_ref.shape[0]
     height = parts * depth
     rows, cols, sizes = rows_ref[...], cols_ref[...], pin_weights_ref[...]
@@ -54,7 +76,8 @@
     lane = iota((LANES + 8, LANES), 0)
     tables, lanes = [], []
     for j in range(rows.shape[0]):
-        fy, fx = fracs_ref[0, j : j + 1, :], fracs_ref[1, j : j + 1, :]
+        cut = slice(j * LANES, (j + 1) * LANES)
+        fy, fx = fracs_ref[0:1, cut], fracs_ref[1:2, cut]
         size, col = sizes[j : j + 1], cols[j : j + 1]
         key = (col >> 7) * depth + rows[j : j + 1]
         tables.append(pick(keys, key, rounded(size * (1.0 - fy)), rounded(size * fy)).astype(bf16))
@@ -65,11 +88,22 @@
         own = total[(t + 1) * height : (t + 2) * height, :LANES]
         spill = total[t * height : (t + 1) * height, LANES : LANES + 1]
         own = own + jnp.where(first_lane, spill, 0.0)
-        out_ref[:height, t * LANES : (t + 1) * LANES] = own.astype(bf16)
+        out_ref[:height, t * LANES : (t + 1) * LANES] = density_codes(own)
     weights = cap_ref[...].astype(f32) * (1.0 - block_ref[...])
-    high, low = halves(weights)
-    rest = jnp.zeros((height - 2 * depth, weights.shape[1]), f32)
-    out_ref[height:, :] = jnp.concatenate([high.astype(f32), low.astype(f32), rest], 0).astype(bf16)
+    code = coded((weights - weight_low) * (1.0 / weight_span))
+    row = iota((height, weights.shape[1]), 0)
+    mine = row // depth == lax.axis_index("cells")
+    out_ref[height:, :] = stored(jnp.where(mine, jnp.concatenate([code] * parts, 0), 0.0))
+
+
+def sum_kernel(sent_ref, out_ref):
+    height = out_ref.shape[0] // 2
+    terms, codes = 0.0, 0.0
+    for base in range(0, sent_ref.shape[0], 2 * height):
+        terms += densities(sent_ref[base : base + height, :])
+        codes += sent_ref[base + height : base + 2 * height, :].astype(f32)
+    out_ref[:height, :] = density_codes(terms)
+    out_ref[height:, :] = stored(codes)
 
 
 def along_lines(values):
@@ -118,7 +152,7 @@
 
 
 def field_kernel(
-    sizes, spot_ref, sent_ref, codes_ref, col_blocks_ref, rows_ref, cols_ref, fracs_ref,
+    sizes, sent_ref, blocks_ref, col_blocks_ref, rows_ref, cols_ref, fracs_ref,
     final_ref, velocity_ref, pairs, weights_ref, source_ref, field_ref,
 ):
     depth, tiles, parts, strips = sizes
@@ -127,39 +161,39 @@
     height = strips * depth
     chunk = min(GROUP, strips) * depth
     chunks = height // chunk
-    strip, part = spot_ref[0], spot_ref[1]
-
-    def unpack(k):
-        code = codes_ref[pl.ds(pl.multiple_of(k * LANES, LANES), LANES), :].astype(f32)
-        high, low = halves((code + code_half) * (block_span / code_top) + block_low)
+    strip, part = lax.axis_index("strip"), lax.axis_index("cells")
+
+    for k in range(pairs.shape[0]):
+        high, low = halves(blocks_ref[k * LANES : (k + 1) * LANES, :])
         pairs[k, :LANES, :] = high
         pairs[k, LANES:, :] = low
 
-    for k in range(pairs.shape[0]):
-        unpack(k)
-
-    sent_rows = 2 * parts * depth
-    span = chunk // depth * parts * sent_rows
-    target, origin = iota((parts * chunk, span), 0), iota((parts * chunk, span), 1)
-    device, slot = origin // sent_rows, origin % sent_rows
-    row_here = target % chunk - (device // parts) * depth
-    side = target // chunk
-    first = parts * depth
-    terms = (slot < first) & (slot // depth == side) & (slot % depth == row_here)
-    pieces = (slot >= first) & (slot < first + 2 * depth) & (device % parts == side) & (slot % depth == row_here)
-    chosen = jnp.concatenate([jnp.where(terms, 1.0, 0.0), jnp.where(pieces, 1.0, 0.0)], 0).astype(bf16)
+    slots = parts * depth
+    group = chunk // depth
+    target, origin = iota((parts * chunk, group * slots), 0), iota((parts * chunk, group * slots), 1)
+    slot = origin % slots
+    fits = (slot // depth == target // chunk) & (origin // slots * depth + slot % depth == target % chunk)
+    chosen = jnp.where(fits, 1.0, 0.0).astype(bf16)
+
+    def placed(values):
+        high, low = halves(jnp.concatenate(values, 0))
+        dot = functools.partial(jnp.dot, preferred_element_type=f32)
+        return dot(chosen, high) + dot(chosen, low)
 
     @functools.partial(each, chunks)
     def place(g):
-        got = jnp.dot(
-            chosen, sent_ref[pl.ds(pl.multiple_of(g * span, span), span), :], preferred_element_type=f32
-        )
+        terms, codes = [], []
+        for n in range(group):
+            base = pl.multiple_of((g * group + n) * (2 * slots), 2 * slots)
+            terms.append(densities(sent_ref[pl.ds(base, slots), :]))
+            codes.append(sent_ref[pl.ds(base + slots, slots), :].astype(f32))
+        term = placed(terms)
+        weight = (placed(codes) + code_half) * (weight_span / code_top) + weight_low
         here = pl.ds(pl.multiple_of(g * chunk, chunk), chunk)
         for p in range(parts):
             cut = slice(p * width_part, (p + 1) * width_part)
-            weight = got[(parts + p) * chunk : (parts + p + 1) * chunk]
-            weights_ref[here, cut] = weight
-            source_ref[here, cut] = got[p * chunk : (p + 1) * chunk] / weight
+            weights_ref[here, cut] = weight[p * chunk : (p + 1) * chunk]
+            source_ref[here, cut] = term[p * chunk : (p + 1) * chunk] / weight[p * chunk : (p + 1) * chunk]
 
     lanes_at_once = width if chunks == 1 else LANES
     col_blocks = [halves(col_blocks_ref[k]) for k in range(col_blocks_ref.shape[0])]
@@ -232,13 +266,13 @@
     rows, cols = rows_ref[...], cols_ref[...]
     keys, lane = iota((many, LANES), 0), iota((LANES + 8, LANES), 0)
     for j in range(rows.shape[0]):
-        fy, fx = fracs_ref[0, j : j + 1, :], fracs_ref[1, j : j + 1, :]
+        cut = slice(j * LANES, (j + 1) * LANES)
+        fy, fx = fracs_ref[0:1, cut], fracs_ref[1:2, cut]
         col = cols[j : j + 1]
         key = (col >> 7) * depth + rows[j : j + 1]
         look = pick(keys, key, rounded(1.0 - fy), rounded(fy)).astype(bf16)
         sampled = jnp.dot(table, look, preferred_element_type=f32)
         share = pick(lane, col & 127, rounded(1.0 - fx), rounded(fx))
-        cut = slice(j * LANES, (j + 1) * LANES)
         velocity_ref[0:1, cut] = jnp.sum(sampled[: LANES + 8] * share, 0, keepdims=True)
         velocity_ref[1:2, cut] = jnp.sum(sampled[LANES + 8 :] * share, 0, keepdims=True)
 
@@ -251,32 +285,32 @@
     pins = pin_rows.shape[0]
     by_lane = (pins // LANES, LANES)
     rows, cols = pin_rows.reshape(by_lane), pin_cols.reshape(by_lane)
-    fracs, sizes = pin_fracs.reshape((2,) + by_lane), pin_weights.reshape(by_lane)
+    sizes = pin_weights.reshape(by_lane)
     vmem = pl.BlockSpec(memory_space=pltpu.VMEM)
     params = pltpu.CompilerParams(vmem_limit_bytes=60 * 1024 * 1024)
 
-    codes = jnp.round((row_blocks - block_low) * (code_top / block_span))
-    codes = (jnp.clip(codes, 0.0, code_top) - code_half).astype(jnp.int16).reshape(-1, LANES)
-    codes = lax.all_gather(codes, "cells", axis=0, tiled=True)
-
-    message = pl.pallas_call(
+    blocks = lax.all_gather(row_blocks.reshape(-1, LANES), "cells", axis=0, tiled=True)
+    carried = jax.ShapeDtypeStruct((2 * parts * depth, width_part), jnp.int16)
+    terms = pl.pallas_call(
         functools.partial(splat_kernel, tiles, parts),
-        out_shape=jax.ShapeDtypeStruct((2 * parts * depth, width_part), bf16),
+        out_shape=carried,
         in_specs=[vmem] * 6,
         out_specs=vmem,
         compiler_params=params,
         name="splat",
-    )(rows, cols, fracs, sizes, capacity, blockage)
-    sent = lax.all_gather(message, ("strip", "cells"), axis=0, tiled=True)
-
-    spot = jnp.stack([lax.axis_index("strip"), lax.axis_index("cells")]).astype(jnp.int32)
+    )(rows, cols, pin_fracs, sizes, capacity, blockage)
+    sums = pl.pallas_call(
+        sum_kernel, out_shape=carried, in_specs=[vmem], out_specs=vmem, compiler_params=params, name="sum_terms"
+    )(lax.all_gather(terms, "cells", axis=0, tiled=True))
+    sent = lax.all_gather(sums, "strip", axis=0, tiled=True)
+
     final, velocity = pl.pallas_call(
         functools.partial(field_kernel, (depth, tiles, parts, strips)),
         out_shape=(
             jax.ShapeDtypeStruct((depth, width_part), f32),
             jax.ShapeDtypeStruct((2, pins), f32),
         ),
-        in_specs=[pl.BlockSpec(memory_space=pltpu.SMEM)] + [vmem] * 6,
+        in_specs=[vmem] * 6,
         out_specs=(vmem, vmem),
         scratch_shapes=[
             pltpu.VMEM((width // LANES, 2 * LANES, LANES), bf16),
@@ -286,7 +320,7 @@
         ],
         compiler_params=params,
         name="field",
-    )(spot, sent, codes, col_blocks, rows, cols, fracs)
+    )(sent, blocks, col_blocks, rows, cols, pin_fracs)
     return final, velocity
 
 

time: 86.4 us -> 71.9 us (0.83)
  waiting for transfers between devices: 45.7 us -> 0.68 us
  blocking collectives: 9.81 us -> 41.9 us
  other arithmetic: 1.68 us -> 0 us
  Pallas kernels: 13.4 us -> 15 us
  local copies, waits for them, and re-layouts: 1.37 us -> 0 us
    all_gather x1, waiting for transfers between devices: 45.7 us -> 0.01 us  [local(): lax.all_gather(row_blocks.reshape(-1, LANES), 'cells', axis=0, tiled=True)]
    all_gather x1 -> x2, blocking collectives: 9.81 us -> 41.9 us  [the longest x1 33.4 us: local(): sent = lax.all_gather(sums, 'strip', axis=0, tiled=True)]
    pallas_call x1 -> x2, Pallas kernels: 2.41 us -> 4.06 us  [the longest x1 2.43 us: local(): pl.pallas_call(functools.partial(splat_kernel, tiles, parts), out_shape=c...]
    unnamed x1 -> x0, local copies, waits for them, and re-layouts: 1.37 us -> none
    convert_element_type x1 -> x0, other arithmetic: 1.09 us -> none  [local(): (jnp.clip(codes, 0.0, code_top) - code_half).astype(jnp.int16)]
  transfers between devices with their start and end apart: 1 -> 1, of which waited for: 1 -> 0; matrix products, arithmetic and copies ran while one was open for 2% -> 0% of each run, Pallas kernels for 0% -> 6%
where the time goes in v2:
time: 71.9 us; the launch traced here: 71.6 us
  blocking collectives  41.9 us (58%)
  Pallas kernels  15 us (21%)
  between operations  14 us (19%)
    all_gather x1, blocking collectives, local(): sent = lax.all_gather(sums, 'strip', axis=0, tiled=True)  33.4 us
    pallas_call x1, Pallas kernels, local(): pl.pallas_call(functools.partial(field_kernel, (depth, tiles, parts, stri...  10.9 us
    all_gather x1, blocking collectives, local(): lax.all_gather(terms, 'cells', axis=0, tiled=True)  8.48 us
    pallas_call x1, Pallas kernels, local(): pl.pallas_call(functools.partial(splat_kernel, tiles, parts), out_shape=c...  2.43 us
    pallas_call x1, Pallas kernels, local(): pl.pallas_call(sum_kernel, out_shape=carried, in_specs=[vmem], out_specs=...  1.63 us
  transfers between devices with their start and end apart: 1, of which 0 were waited for; matrix products, arithmetic and copies ran while one was open for 0% of the time, Pallas kernels for 6%

profile of v2, /device:TPU:0, one launch (start us, length us, event | category | flops | bytes accessed | tf_op | source)
XLA Modules:
  0.0 71.6 jit_solution(14925224100895036505)
XLA Ops:
  7.2 0.0 all-gather.2.cloned.1.call-start
  7.2 0.7 all-gather.2.cloned.1.call-update
  7.9 2.4 %splat.1 = s16[32,640]{1,0:T(8,128)(2,1)} custom-call(s32[32,128]{1,0:T(8,128)} %bitcast.5, s32[32,128]{1,0:T(8,128)} %bitcast.7, f32[2,4096]{1,0:T(2,128)} %fracs_ref.3, f32[32,128]{1,0:T(8,128)} %bitcast.9, s32[4,640]{1,0:T(4,128)} %cap_ref.1, f32[4,640]{1,0:T(4,128)} %block_ref.1), custom_call_target="tpu_custom_call" | custom-call | tf_op jit(solution)/shard_map/splat/pallas_call | solution.py:294
  10.3 8.5 %all_gather.9.sent_ref = s16[128,640]{1,0:T(8,128)(2,1)} all-gather(s16[32,640]{1,0:T(8,128)(2,1)} %splat.1), channel_id=1, replica_groups=mesh['strip'=8,'cells'=4] {'cells'}, dimensions={0}, use_global_device_ids=true | all-gather | bytes 204800 | tf_op jit(solution)/shard_map/all_gather | solution.py:304
  18.8 1.6 %sum_terms.1 = s16[32,640]{1,0:T(8,128)(2,1)} custom-call(s16[128,640]{1,0:T(8,128)(2,1)} %all_gather.9.sent_ref), custom_call_target="tpu_custom_call" | custom-call | tf_op jit(solution)/shard_map/sum_terms/pallas_call | solution.py:302
  20.4 33.4 %all_gather.10.sent_ref = s16[256,640]{1,0:T(8,128)(2,1)} all-gather(s16[32,640]{1,0:T(8,128)(2,1)} %sum_terms.1), channel_id=1, replica_groups=mesh['strip'=8,'cells'=4] {'strip'}, dimensions={0}, use_global_device_ids=true | all-gather | bytes 368640 | tf_op jit(solution)/shard_map/all_gather | solution.py:305
  53.8 0.0 all-gather.2.cloned.1.call-done.blocks_ref
  53.8 10.9 %field.1 = (f32[4,640]{1,0:T(4,128)}, f32[2,4096]{1,0:T(2,128)}) custom-call(s16[256,640]{1,0:T(8,128)(2,1)} %all_gather.10.sent_ref, f32[2560,128]{1,0:T(8,128)} %all-gather.2.cloned.1.call-done.blocks_ref, f32[1,32,32]{2,1,0:T(8,128)} %col_blocks_ref.1, s32[32,128]{1,0:T(8,128)} %bitcast.6, s32[32,128]{1,0:T(8,128)} %bitcast.8, f32[2,4096]{1,0:T(2,128)} %fracs_ref.3), custom_call_target="tpu_custom_call" | custom-call | tf_op jit(solution)/shard_map/field/pallas_call | solution.py:307
Async XLA Ops:
  7.2 46.7 %all-gather.2.cloned.1.call-start = ((), (), s32[]{:S(2)}) async-start(), calls=%async_computation | async-start | bytes 1638400 | tf_op jit(solution)/shard_map/all_gather | solution.py:292
Sparse Core Ops, SparseCore 0:
  9.6 20.8 all-gather.1

commit v3 on v2

--- a/solution.py
+++ b/solution.py
@@ -97,13 +97,19 @@
 
 
 def sum_kernel(sent_ref, out_ref):
-    height = out_ref.shape[0] // 2
+    rows = out_ref.shape[1]
+    height = rows // 2
     terms, codes = 0.0, 0.0
-    for base in range(0, sent_ref.shape[0], 2 * height):
+    for base in range(0, sent_ref.shape[0], rows):
         terms += densities(sent_ref[base : base + height, :])
-        codes += sent_ref[base + height : base + 2 * height, :].astype(f32)
-    out_ref[:height, :] = density_codes(terms)
-    out_ref[height:, :] = stored(codes)
+        codes += sent_ref[base + height : base + rows, :].astype(f32)
+    message = jnp.concatenate([density_codes(terms), stored(codes)], 0)
+
+    def write(n):
+        out_ref[n] = message
+
+    for n in range(out_ref.shape[0]):
+        write(n)
 
 
 def along_lines(values):
@@ -300,9 +306,14 @@
         name="splat",
     )(rows, cols, pin_fracs, sizes, capacity, blockage)
     sums = pl.pallas_call(
-        sum_kernel, out_shape=carried, in_specs=[vmem], out_specs=vmem, compiler_params=params, name="sum_terms"
+        sum_kernel,
+        out_shape=jax.ShapeDtypeStruct((strips,) + carried.shape, jnp.int16),
+        in_specs=[vmem],
+        out_specs=vmem,
+        compiler_params=params,
+        name="sum_terms",
     )(lax.all_gather(terms, "cells", axis=0, tiled=True))
-    sent = lax.all_gather(sums, "strip", axis=0, tiled=True)
+    sent = lax.all_to_all(sums, "strip", split_axis=0, concat_axis=0, tiled=True).reshape(-1, width_part)
 
     final, velocity = pl.pallas_call(
         functools.partial(field_kernel, (depth, tiles, parts, strips)),

time: 71.9 us -> 56.1 us (0.78)
  blocking collectives: 41.9 us -> 25.8 us
    all_gather x1 -> x0, blocking collectives: 33.4 us -> none  [local(): sent = lax.all_gather(sums, 'strip', axis=0, tiled=True)]
    all_to_all x0 -> x1, blocking collectives: none -> 17.3 us  [local(): lax.all_to_all(sums, 'strip', split_axis=0, concat_axis=0, tiled=True)]
  transfers between devices with their start and end apart: 1 -> 1, of which waited for: 0 -> 0; matrix products, arithmetic and copies ran while one was open for 0% -> 0% of each run, Pallas kernels for 6% -> 7%
where the time goes in v3:
time: 56.1 us; the launch traced here: 55.7 us
  blocking collectives  25.8 us (46%)
  Pallas kernels  15.1 us (27%)
  between operations  14 us (25%)
  waiting for transfers between devices  0.68 us (1%)
    all_to_all x1, blocking collectives, local(): lax.all_to_all(sums, 'strip', split_axis=0, concat_axis=0, tiled=True)  17.3 us
    pallas_call x1, Pallas kernels, local(): pl.pallas_call(functools.partial(field_kernel, (depth, tiles, parts, stri...  10.9 us
    all_gather x1, blocking collectives, local(): lax.all_gather(terms, 'cells', axis=0, tiled=True)  8.48 us
    pallas_call x1, Pallas kernels, local(): pl.pallas_call(functools.partial(splat_kernel, tiles, parts), out_shape=c...  2.43 us
    pallas_call x1, Pallas kernels, local(): pl.pallas_call(sum_kernel, out_shape=jax.ShapeDtypeStruct((strips,) + car...  1.75 us
  transfers between devices with their start and end apart: 1, of which 0 were waited for; matrix products, arithmetic and copies ran while one was open for 0% of the time, Pallas kernels for 7%

profile of v3, /device:TPU:0, one launch (start us, length us, event | category | flops | bytes accessed | tf_op | source)
XLA Modules:
  0.0 55.7 jit_solution(17234697991517344180)
XLA Ops:
  7.2 0.0 all-gather.2.cloned.1.call-start
  7.2 0.7 %all-gather.2.cloned.1.call-update = ((f32[640,128]{1,0:T(8,128)}), f32[2560,128]{1,0:T(8,128)}) async-update(((), (), s32[]{:S(2)}) %all-gather.2.cloned.1.call-start, f32[640,128]{1,0:T(8,128)} %bitcast.6) | async-update | bytes 1966104
  7.9 2.4 %splat.1 = s16[32,640]{1,0:T(8,128)(2,1)} custom-call(s32[32,128]{1,0:T(8,128)} %bitcast.7, s32[32,128]{1,0:T(8,128)} %bitcast.9, f32[2,4096]{1,0:T(2,128)} %fracs_ref.3, f32[32,128]{1,0:T(8,128)} %bitcast.11, s32[4,640]{1,0:T(4,128)} %cap_ref.1, f32[4,640]{1,0:T(4,128)} %block_ref.1), custom_call_target="tpu_custom_call" | custom-call | tf_op jit(solution)/shard_map/splat/pallas_call | solution.py:300
  10.3 8.5 %all_gather.6.sent_ref = s16[128,640]{1,0:T(8,128)(2,1)} all-gather(s16[32,640]{1,0:T(8,128)(2,1)} %splat.1), channel_id=1, replica_groups=mesh['strip'=8,'cells'=4] {'cells'}, dimensions={0}, use_global_device_ids=true | all-gather | bytes 204800 | tf_op jit(solution)/shard_map/all_gather | solution.py:315
  18.8 1.7 %sum_terms.1 = s16[8,32,640]{2,1,0:T(8,128)(2,1)} custom-call(s16[128,640]{1,0:T(8,128)(2,1)} %all_gather.6.sent_ref), custom_call_target="tpu_custom_call" | custom-call | tf_op jit(solution)/shard_map/sum_terms/pallas_call | solution.py:308
  20.6 17.3 %all_to_all.5 = s16[8,32,640]{2,1,0:T(8,128)(2,1)} all-to-all(s16[8,32,640]{2,1,0:T(8,128)(2,1)} %sum_terms.1), channel_id=1, replica_groups=mesh['strip'=8,'cells'=4] {'strip'}, dimensions={0} | all-to-all | bytes 655360 | tf_op jit(solution)/shard_map/all_to_all | solution.py:316
  37.9 0.0 all-gather.2.cloned.1.call-done.blocks_ref
  37.9 10.9 %field.1 = (f32[4,640]{1,0:T(4,128)}, f32[2,4096]{1,0:T(2,128)}) custom-call(s16[256,640]{1,0:T(8,128)(2,1)} %bitcast.5, f32[2560,128]{1,0:T(8,128)} %all-gather.2.cloned.1.call-done.blocks_ref, f32[1,32,32]{2,1,0:T(8,128)} %col_blocks_ref.1, s32[32,128]{1,0:T(8,128)} %bitcast.8, s32[32,128]{1,0:T(8,128)} %bitcast.10, f32[2,4096]{1,0:T(2,128)} %fracs_ref.3), custom_call_target="tpu_custom_call" | custom-call | tf_op jit(solution)/shard_map/field/pallas_call | solution.py:318
Async XLA Ops:
  7.2 30.7 %all-gather.2.cloned.1.call-start = ((), (), s32[]{:S(2)}) async-start(), calls=%async_computation.1 | async-start | bytes 1638400 | tf_op jit(solution)/shard_map/all_gather | solution.py:298
Sparse Core Ops, SparseCore 0:
  9.6 20.8 all-gather.1

commit v4 on v3

--- a/solution.py
+++ b/solution.py
@@ -14,6 +14,7 @@
 
 coupling = 2.0
 floor_level = 0.5
+block_low, block_span = -0.002, 0.152
 weight_low, weight_span = 0.5, 3.5
 term_low, term_octaves = -20.0, 34.0
 code_top = 65535.0
@@ -65,7 +66,7 @@
 
 
 def splat_kernel(
-    tiles, parts, rows_ref, cols_ref, fracs_ref, pin_weights_ref, cap_ref, block_ref, out_ref
+    tiles, parts, rows_ref, cols_ref, fracs_ref, pin_weights_ref, cap_ref, block_ref, row_blocks_ref, out_ref
 ):
     depth = cap_ref.shape[0]
     height = parts * depth
@@ -88,21 +89,24 @@
         own = total[(t + 1) * height : (t + 2) * height, :LANES]
         spill = total[t * height : (t + 1) * height, LANES : LANES + 1]
         own = own + jnp.where(first_lane, spill, 0.0)
-        out_ref[:height, t * LANES : (t + 1) * LANES] = density_codes(own)
+        cut = slice(t * LANES, (t + 1) * LANES)
+        out_ref[:height, cut] = density_codes(own)
+        share = (row_blocks_ref[t * LANES : (t + 1) * LANES, :] - block_low) * (1.0 / block_span)
+        out_ref[2 * height :, cut] = stored(coded(share))
     weights = cap_ref[...].astype(f32) * (1.0 - block_ref[...])
     code = coded((weights - weight_low) * (1.0 / weight_span))
     row = iota((height, weights.shape[1]), 0)
     mine = row // depth == lax.axis_index("cells")
-    out_ref[height:, :] = stored(jnp.where(mine, jnp.concatenate([code] * parts, 0), 0.0))
-
-
-def sum_kernel(sent_ref, out_ref):
-    rows = out_ref.shape[1]
-    height = rows // 2
+    out_ref[height : 2 * height, :] = stored(jnp.where(mine, jnp.concatenate([code] * parts, 0), 0.0))
+
+
+def sum_kernel(*refs):
+    sent_refs, out_ref = refs[:-1], refs[-1]
+    height = out_ref.shape[1] // 2
     terms, codes = 0.0, 0.0
-    for base in range(0, sent_ref.shape[0], rows):
-        terms += densities(sent_ref[base : base + height, :])
-        codes += sent_ref[base + height : base + rows, :].astype(f32)
+    for sent_ref in sent_refs:
+        terms += densities(sent_ref[:height, :])
+        codes += sent_ref[height:, :].astype(f32)
     message = jnp.concatenate([density_codes(terms), stored(codes)], 0)
 
     def write(n):
@@ -170,7 +174,9 @@
     strip, part = lax.axis_index("strip"), lax.axis_index("cells")
 
     for k in range(pairs.shape[0]):
-        high, low = halves(blocks_ref[k * LANES : (k + 1) * LANES, :])
+        base = (k // tiles) * (2 * parts * depth + LANES) + 2 * parts * depth
+        code = blocks_ref[base : base + LANES, k % tiles * LANES : (k % tiles + 1) * LANES].astype(f32)
+        high, low = halves((code + code_half) * (block_span / code_top) + block_low)
         pairs[k, :LANES, :] = high
         pairs[k, LANES:, :] = low
 
@@ -295,24 +301,30 @@
     vmem = pl.BlockSpec(memory_space=pltpu.VMEM)
     params = pltpu.CompilerParams(vmem_limit_bytes=60 * 1024 * 1024)
 
-    blocks = lax.all_gather(row_blocks.reshape(-1, LANES), "cells", axis=0, tiled=True)
-    carried = jax.ShapeDtypeStruct((2 * parts * depth, width_part), jnp.int16)
+    carried = 2 * parts * depth
     terms = pl.pallas_call(
         functools.partial(splat_kernel, tiles, parts),
-        out_shape=carried,
-        in_specs=[vmem] * 6,
+        out_shape=jax.ShapeDtypeStruct((carried + LANES, width_part), jnp.int16),
+        in_specs=[vmem] * 7,
         out_specs=vmem,
         compiler_params=params,
         name="splat",
-    )(rows, cols, pin_fracs, sizes, capacity, blockage)
+    )(rows, cols, pin_fracs, sizes, capacity, blockage, row_blocks.reshape(-1, LANES))
+    blocks = lax.all_gather(terms, "cells", axis=0, tiled=True)
+
+    def terms_of(part):
+        place = part * (carried + LANES) // carried
+        return pl.BlockSpec((carried, width_part), lambda i: (place, 0))
+
     sums = pl.pallas_call(
         sum_kernel,
-        out_shape=jax.ShapeDtypeStruct((strips,) + carried.shape, jnp.int16),
-        in_specs=[vmem],
-        out_specs=vmem,
+        grid=(1,),
+        out_shape=jax.ShapeDtypeStruct((strips, carried, width_part), jnp.int16),
+        in_specs=[terms_of(part) for part in range(parts)],
+        out_specs=pl.BlockSpec((strips, carried, width_part), lambda i: (0, 0, 0)),
         compiler_params=params,
         name="sum_terms",
-    )(lax.all_gather(terms, "cells", axis=0, tiled=True))
+    )(*[blocks] * parts)
     sent = lax.all_to_all(sums, "strip", split_axis=0, concat_axis=0, tiled=True).reshape(-1, width_part)
 
     final, velocity = pl.pallas_call(

time: 56.1 us -> 45.5 us (0.81)
  between operations: 14 us -> 0.63 us
  blocking collectives: 25.8 us -> 29.2 us
  waiting for transfers between devices: 0.68 us -> 0 us
    all_gather x1, blocking collectives: 8.48 us -> 11.8 us  [local(): blocks = lax.all_gather(terms, 'cells', axis=0, tiled=True)]
    unnamed x1 -> x0, waiting for transfers between devices: 0.68 us -> none
  transfers between devices with their start and end apart: 1 -> 0, of which waited for: 0 -> 0; matrix products, arithmetic and copies ran while one was open for 0% -> 0% of each run, Pallas kernels for 7% -> 0%
where the time goes in v4:
time: 45.5 us; the launch traced here: 45.2 us
  blocking collectives  29.2 us (64%)
  Pallas kernels  15.4 us (34%)
  between operations  0.63 us (1%)
    all_to_all x1, blocking collectives, local(): lax.all_to_all(sums, 'strip', split_axis=0, concat_axis=0, tiled=True)  17.3 us
    all_gather x1, blocking collectives, local(): blocks = lax.all_gather(terms, 'cells', axis=0, tiled=True)  11.8 us
    pallas_call x1, Pallas kernels, local(): pl.pallas_call(functools.partial(field_kernel, (depth, tiles, parts, stri...  10.9 us
    pallas_call x1, Pallas kernels, local(): pl.pallas_call(functools.partial(splat_kernel, tiles, parts), out_shape=j...  2.84 us
    pallas_call x1, Pallas kernels, local(): pl.pallas_call(sum_kernel, grid=(1,), out_shape=jax.ShapeDtypeStruct((str...  1.67 us

profile of v4, /device:TPU:0, one launch (start us, length us, event | category | flops | bytes accessed | tf_op | source)
XLA Modules:
  0.0 45.2 jit_solution(4741575938338286476)
XLA Ops:
  0.6 2.8 %splat.1 = s16[160,640]{1,0:T(8,128)(2,1)} custom-call(s32[32,128]{1,0:T(8,128)} %bitcast.7, s32[32,128]{1,0:T(8,128)} %bitcast.9, f32[2,4096]{1,0:T(2,128)} %fracs_ref.3, f32[32,128]{1,0:T(8,128)} %bitcast.11, s32[4,640]{1,0:T(4,128)} %cap_ref.1, f32[4,640]{1,0:T(4,128)} %block_ref.1, f32[640,128]{1,0:T(8,128)} %bitcast.6), custom_call_target="tpu_custom_call" | custom-call | tf_op jit(solution)/shard_map/splat/pallas_call | solution.py:305
  3.5 11.8 %all_gather.3.refs_0_.refs_1_.refs_2_.refs_3_.blocks_ref = s16[640,640]{1,0:T(8,128)(2,1)} all-gather(s16[160,640]{1,0:T(8,128)(2,1)} %splat.1), channel_id=1, replica_groups=mesh['strip'=8,'cells'=4] {'cells'}, dimensions={0}, use_global_device_ids=true | all-gather | bytes 1024000 | tf_op jit(solution)/shard_map/all_gather | solution.py:313
  15.3 1.7 %sum_terms.1 = s16[8,32,640]{2,1,0:T(8,128)(2,1)} custom-call(s16[640,640]{1,0:T(8,128)(2,1)} %all_gather.3.refs_0_.refs_1_.refs_2_.refs_3_.blocks_ref, s16[640,640]{1,0:T(8,128)(2,1)} %all_gather.3.refs_0_.refs_1_.refs_2_.refs_3_.blocks_ref, s16[640,640]{1,0:T(8,128)(2,1)} %all_gather.3.refs_0_.refs_1_.refs_2_.refs_3_.blocks_ref, ...), custom_call_target="tpu_custom_call" | custom-call | tf_op jit(solution)/shard_map/sum_terms/pallas_call | solution.py:319
  17.0 17.3 %all_to_all.5 = s16[8,32,640]{2,1,0:T(8,128)(2,1)} all-to-all(s16[8,32,640]{2,1,0:T(8,128)(2,1)} %sum_terms.1), channel_id=1, replica_groups=mesh['strip'=8,'cells'=4] {'strip'}, dimensions={0} | all-to-all | bytes 655360 | tf_op jit(solution)/shard_map/all_to_all | solution.py:328
  34.3 10.9 %field.1 = (f32[4,640]{1,0:T(4,128)}, f32[2,4096]{1,0:T(2,128)}) custom-call(s16[256,640]{1,0:T(8,128)(2,1)} %bitcast.5, s16[640,640]{1,0:T(8,128)(2,1)} %all_gather.3.refs_0_.refs_1_.refs_2_.refs_3_.blocks_ref, f32[1,32,32]{2,1,0:T(8,128)} %col_blocks_ref.1, s32[32,128]{1,0:T(8,128)} %bitcast.8, s32[32,128]{1,0:T(8,128)} %bitcast.10, f32[2,4096]{1,0:T(2,128)} %fracs_ref.3), custom_call_target="tpu_custom_call" | custom-call | tf_op jit(solution)/shard_map/field/pallas_call | solution.py:330

commit v5 on v4

--- a/solution.py
+++ b/solution.py
@@ -102,18 +102,13 @@
 
 def sum_kernel(*refs):
     sent_refs, out_ref = refs[:-1], refs[-1]
-    height = out_ref.shape[1] // 2
+    height = out_ref.shape[0] // 2
     terms, codes = 0.0, 0.0
     for sent_ref in sent_refs:
         terms += densities(sent_ref[:height, :])
         codes += sent_ref[height:, :].astype(f32)
-    message = jnp.concatenate([density_codes(terms), stored(codes)], 0)
-
-    def write(n):
-        out_ref[n] = message
-
-    for n in range(out_ref.shape[0]):
-        write(n)
+    out_ref[:height, :] = density_codes(terms)
+    out_ref[height:, :] = stored(codes)
 
 
 def along_lines(values):
@@ -162,10 +157,10 @@
 
 
 def field_kernel(
-    sizes, sent_ref, blocks_ref, col_blocks_ref, rows_ref, cols_ref, fracs_ref,
-    final_ref, velocity_ref, pairs, weights_ref, source_ref, field_ref,
+    sizes, blocks_ref, col_blocks_ref, rows_ref, cols_ref, fracs_ref, *refs,
 ):
     depth, tiles, parts, strips = sizes
+    sent_refs, (final_ref, velocity_ref, pairs, weights_ref, source_ref, field_ref, ordered) = refs[:-7], refs[-7:]
     width_part = tiles * LANES
     width = parts * width_part
     height = strips * depth
@@ -181,6 +176,12 @@
         pairs[k, LANES:, :] = low
 
     slots = parts * depth
+    if len(sent_refs) == 1:
+        sent = sent_refs[0]
+    else:
+        sent = ordered
+        for k, sent_ref in enumerate(sent_refs):
+            ordered[strip ^ k] = sent_ref[...]
     group = chunk // depth
     target, origin = iota((parts * chunk, group * slots), 0), iota((parts * chunk, group * slots), 1)
     slot = origin % slots
@@ -196,9 +197,9 @@
     def place(g):
         terms, codes = [], []
         for n in range(group):
-            base = pl.multiple_of((g * group + n) * (2 * slots), 2 * slots)
-            terms.append(densities(sent_ref[pl.ds(base, slots), :]))
-            codes.append(sent_ref[pl.ds(base + slots, slots), :].astype(f32))
+            got = sent[g * group + n]
+            terms.append(densities(got[:slots]))
+            codes.append(got[slots:].astype(f32))
         term = placed(terms)
         weight = (placed(codes) + code_half) * (weight_span / code_top) + weight_low
         here = pl.ds(pl.multiple_of(g * chunk, chunk), chunk)
@@ -299,7 +300,9 @@
     rows, cols = pin_rows.reshape(by_lane), pin_cols.reshape(by_lane)
     sizes = pin_weights.reshape(by_lane)
     vmem = pl.BlockSpec(memory_space=pltpu.VMEM)
-    params = pltpu.CompilerParams(vmem_limit_bytes=60 * 1024 * 1024)
+    small = pltpu.CompilerParams(vmem_limit_bytes=16 * 1024 * 1024)
+    grid_bytes = 4 * height * width
+    large = pltpu.CompilerParams(vmem_limit_bytes=(20 << 20) + 6 * grid_bytes)
 
     carried = 2 * parts * depth
     terms = pl.pallas_call(
@@ -307,7 +310,7 @@
         out_shape=jax.ShapeDtypeStruct((carried + LANES, width_part), jnp.int16),
         in_specs=[vmem] * 7,
         out_specs=vmem,
-        compiler_params=params,
+        compiler_params=small,
         name="splat",
     )(rows, cols, pin_fracs, sizes, capacity, blockage, row_blocks.reshape(-1, LANES))
     blocks = lax.all_gather(terms, "cells", axis=0, tiled=True)
@@ -319,13 +322,18 @@
     sums = pl.pallas_call(
         sum_kernel,
         grid=(1,),
-        out_shape=jax.ShapeDtypeStruct((strips, carried, width_part), jnp.int16),
+        out_shape=jax.ShapeDtypeStruct((carried, width_part), jnp.int16),
         in_specs=[terms_of(part) for part in range(parts)],
-        out_specs=pl.BlockSpec((strips, carried, width_part), lambda i: (0, 0, 0)),
-        compiler_params=params,
+        out_specs=pl.BlockSpec((carried, width_part), lambda i: (0, 0)),
+        compiler_params=small,
         name="sum_terms",
     )(*[blocks] * parts)
-    sent = lax.all_to_all(sums, "strip", split_axis=0, concat_axis=0, tiled=True).reshape(-1, width_part)
+    if strips == 8:
+        sent = [sums] + [None] * 7
+        for k in (6, 7, 4, 5, 2, 3, 1):
+            sent[k] = lax.ppermute(sums, "strip", [(n, n ^ k) for n in range(strips)])
+    else:
+        sent = [lax.all_gather(sums, "strip", axis=0)]
 
     final, velocity = pl.pallas_call(
         functools.partial(field_kernel, (depth, tiles, parts, strips)),
@@ -333,17 +341,18 @@
             jax.ShapeDtypeStruct((depth, width_part), f32),
             jax.ShapeDtypeStruct((2, pins), f32),
         ),
-        in_specs=[vmem] * 6,
+        in_specs=[vmem] * (5 + len(sent)),
         out_specs=(vmem, vmem),
         scratch_shapes=[
             pltpu.VMEM((width // LANES, 2 * LANES, LANES), bf16),
             pltpu.VMEM((height, width), f32),
             pltpu.VMEM((height, width), f32),
             pltpu.VMEM((height + 16, width), f32),
+            pltpu.VMEM((len(sent), carried, width_part), jnp.int16),
         ],
-        compiler_params=params,
+        compiler_params=large,
         name="field",
-    )(sent, blocks, col_blocks, rows, cols, pin_fracs)
+    )(blocks, col_blocks, rows, cols, pin_fracs, *sent)
     return final, velocity
 
 

time: 45.5 us -> 42.4 us (0.932)
  blocking collectives: 29.2 us -> 10.3 us
  starting transfers between devices: 0 us -> 11.2 us
  local copies, waits for them, and re-layouts: 0 us -> 5.29 us
  Pallas kernels: 15.4 us -> 10.9 us
  waiting for transfers between devices: 0 us -> 3.47 us
    all_to_all x1 -> x0, blocking collectives: 17.3 us -> none  [local(): lax.all_to_all(sums, 'strip', split_axis=0, concat_axis=0, tiled=True)]
    ppermute x0 -> x7, starting transfers between devices: none -> 11.2 us  [local(): sent[k] = lax.ppermute(sums, 'strip', [(n, n ^ k) for n in range(strips)])]
    unnamed x0 -> x22, local copies, waits for them, and re-layouts: none -> 5.29 us
    ppermute x0 -> x7, waiting for transfers between devices: none -> 3.47 us  [local(): sent[k] = lax.ppermute(sums, 'strip', [(n, n ^ k) for n in range(strips)])]
    pallas_call x1, Pallas kernels: 2.84 us -> 1.14 us  [local(): pl.pallas_call(functools.partial(splat_kernel, tiles, parts), out_shape=j...]
    all_gather x1, blocking collectives: 11.8 us -> 10.3 us  [local(): blocks = lax.all_gather(terms, 'cells', axis=0, tiled=True)]
    pallas_call x1, Pallas kernels: 1.67 us -> 0.1 us  [local(): pl.pallas_call(sum_kernel, grid=(1,), out_shape=jax.ShapeDtypeStruct((car...]
    pallas_call x1, Pallas kernels: 10.9 us -> 9.67 us  [local(): pl.pallas_call(functools.partial(field_kernel, (depth, tiles, parts, stri...]
  transfers between devices with their start and end apart: 0 -> 7, of which waited for: 0 -> 5; matrix products, arithmetic and copies ran while one was open for 0% -> 0% of each run, Pallas kernels for 0% -> 0%
where the time goes in v5:
time: 42.4 us; the launch traced here: 41.8 us
  starting transfers between devices  11.2 us (26%)
  Pallas kernels  10.9 us (26%)
  blocking collectives  10.3 us (24%)
  local copies, waits for them, and re-layouts  5.29 us (12%)
  waiting for transfers between devices  3.47 us (8%)
  between operations  0.68 us (2%)
    ppermute x7, starting transfers between devices, local(): sent[k] = lax.ppermute(sums, 'strip', [(n, n ^ k) for n in range(strips)])  11.2 us
    all_gather x1, blocking collectives, local(): blocks = lax.all_gather(terms, 'cells', axis=0, tiled=True)  10.3 us
    pallas_call x1, Pallas kernels, local(): pl.pallas_call(functools.partial(field_kernel, (depth, tiles, parts, stri...  9.67 us
    unnamed x22, local copies, waits for them, and re-layouts  5.29 us
    ppermute x7, waiting for transfers between devices, local(): sent[k] = lax.ppermute(sums, 'strip', [(n, n ^ k) for n in range(strips)])  3.47 us
    pallas_call x1, Pallas kernels, local(): pl.pallas_call(functools.partial(splat_kernel, tiles, parts), out_shape=j...  1.14 us
  transfers between devices with their start and end apart: 7, of which 5 were waited for; matrix products, arithmetic and copies ran while one was open for 0% of the time, Pallas kernels for 0%

profile of v5, /device:TPU:0, one launch (start us, length us, event | category | flops | bytes accessed | tf_op | source)
XLA Modules:
  0.0 41.8 jit_solution(13613682038675999783)
XLA Ops:
  0.6 1.0 %copy-done = f32[5,128,128]{2,1,0:T(8,128)S(1)} copy-done((f32[5,128,128]{2,1,0:T(8,128)S(1)}, f32[5,128,128]{2,1,0:T(8,128)}, u32[]{:S(2)}) %copy-start) | copy-done | bytes 327704
  1.6 0.8 %copy-done.1 = f32[2,4096]{1,0:T(2,128)S(1)} copy-done((f32[2,4096]{1,0:T(2,128)S(1)}, f32[2,4096]{1,0:T(2,128)}, u32[]{:S(2)}) %copy-start.1) | copy-done | bytes 32792
  2.4 0.7 %copy-done.3 = s32[4096]{0:T(1024)S(1)} copy-done((s32[4096]{0:T(1024)S(1)}, s32[4096]{0:T(1024)}, u32[]{:S(2)}) %copy-start.3) | copy-done | bytes 16408
  3.1 0.7 %copy-done.5 = s32[4096]{0:T(1024)S(1)} copy-done((s32[4096]{0:T(1024)S(1)}, s32[4096]{0:T(1024)}, u32[]{:S(2)}) %copy-start.5) | copy-done | bytes 16408
  3.8 0.7 %copy-done.8 = f32[4096]{0:T(1024)S(1)} copy-done((f32[4096]{0:T(1024)S(1)}, f32[4096]{0:T(1024)}, u32[]{:S(2)}) %copy-start.8) | copy-done | bytes 16408
  4.5 0.7 %copy-done.9 = s32[4,640]{1,0:T(4,128)S(1)} copy-done((s32[4,640]{1,0:T(4,128)S(1)}, s32[4,640]{1,0:T(4,128)}, u32[]{:S(2)}) %copy-start.9) | copy-done | bytes 10264
  5.2 0.7 %copy-done.10 = f32[4,640]{1,0:T(4,128)S(1)} copy-done((f32[4,640]{1,0:T(4,128)S(1)}, f32[4,640]{1,0:T(4,128)}, u32[]{:S(2)}) %copy-start.10) | copy-done | bytes 10264
  5.9 1.1 %splat.1 = s16[160,640]{1,0:T(8,128)(2,1)S(1)} custom-call(s32[32,128]{1,0:T(8,128)S(1)} %bitcast.5, s32[32,128]{1,0:T(8,128)S(1)} %bitcast.7, f32[2,4096]{1,0:T(2,128)S(1)} %copy-done.1, f32[32,128]{1,0:T(8,128)S(1)} %bitcast.9, s32[4,640]{1,0:T(4,128)S(1)} %copy-done.9, f32[4,640]{1,0:T(4,128)S(1)} %copy-done.10, f32[640,128]{1,0:T(8,128)S(1)} %bitcast.4), custom_call_target="tpu_custom_call" | custom-call | tf_op jit(solution)/shard_map/splat/pallas_call | solution.py:308
  7.1 10.3 %all_gather.3.refs_0_.refs_1_.refs_2_.refs_3_.blocks_ref = s16[640,640]{1,0:T(8,128)(2,1)S(1)} all-gather(s16[160,640]{1,0:T(8,128)(2,1)S(1)} %splat.1), channel_id=1, replica_groups=mesh['strip'=8,'cells'=4] {'cells'}, dimensions={0}, use_global_device_ids=true | all-gather | bytes 1024000 | tf_op jit(solution)/shard_map/all_gather | solution.py:316
  17.3 0.1 sum_terms.1.refs_0_
  17.4 4.6 %collective-permute-start.6 = (s16[32,640]{1,0:T(8,128)(2,1)S(1)}, s16[32,640]{1,0:T(8,128)(2,1)S(1)}, u32[]{:S(2)}, u32[]{:S(2)}) collective-permute-start(s16[32,640]{1,0:T(8,128)(2,1)S(1)} %sum_terms.1.refs_0_), channel_id=1, source_target_pairs={{0,28},{4,24},{8,20},{12,16},{16,12},{20,8},{24,4},{28,0},{1,29},{... | collective-permute-start | bytes 122888 | tf_op jit(solution)/shard_map/ppermute | solution.py:334
  22.0 0.2 collective-permute-start.5
  22.3 0.8 %collective-permute-start.4 = (s16[32,640]{1,0:T(8,128)(2,1)S(1)}, s16[32,640]{1,0:T(8,128)(2,1)S(1)}, u32[]{:S(2)}, u32[]{:S(2)}) collective-permute-start(s16[32,640]{1,0:T(8,128)(2,1)S(1)} %sum_terms.1.refs_0_), channel_id=1, source_target_pairs={{0,20},{4,16},{8,28},{12,24},{16,4},{20,0},{24,12},{28,8},{1,21},{... | collective-permute-start | bytes 122888 | tf_op jit(solution)/shard_map/ppermute | solution.py:334
  23.0 2.1 %collective-permute-start.3 = (s16[32,640]{1,0:T(8,128)(2,1)S(1)}, s16[32,640]{1,0:T(8,128)(2,1)S(1)}, u32[]{:S(2)}, u32[]{:S(2)}) collective-permute-start(s16[32,640]{1,0:T(8,128)(2,1)S(1)} %sum_terms.1.refs_0_), channel_id=1, source_target_pairs={{0,16},{4,20},{8,24},{12,28},{16,0},{20,4},{24,8},{28,12},{1,17},{... | collective-permute-start | bytes 122888 | tf_op jit(solution)/shard_map/ppermute | solution.py:334
  25.2 2.2 %collective-permute-start.2 = (s16[32,640]{1,0:T(8,128)(2,1)S(1)}, s16[32,640]{1,0:T(8,128)(2,1)S(1)}, u32[]{:S(2)}, u32[]{:S(2)}) collective-permute-start(s16[32,640]{1,0:T(8,128)(2,1)S(1)} %sum_terms.1.refs_0_), channel_id=1, source_target_pairs={{0,12},{4,8},{8,4},{12,0},{16,28},{20,24},{24,20},{28,16},{1,13},{... | collective-permute-start | bytes 122888 | tf_op jit(solution)/shard_map/ppermute | solution.py:334
  27.3 0.0 collective-permute-done.6.refs_7_
  27.3 0.8 %collective-permute-start.1 = (s16[32,640]{1,0:T(8,128)(2,1)S(1)}, s16[32,640]{1,0:T(8,128)(2,1)S(1)}, u32[]{:S(2)}, u32[]{:S(2)}) collective-permute-start(s16[32,640]{1,0:T(8,128)(2,1)S(1)} %sum_terms.1.refs_0_), channel_id=1, source_target_pairs={{0,8},{4,12},{8,0},{12,4},{16,24},{20,28},{24,16},{28,20},{1,9},{5... | collective-permute-start | bytes 122888 | tf_op jit(solution)/shard_map/ppermute | solution.py:334
  28.1 0.5 %collective-permute-start = (s16[32,640]{1,0:T(8,128)(2,1)S(1)}, s16[32,640]{1,0:T(8,128)(2,1)S(1)}, u32[]{:S(2)}, u32[]{:S(2)}) collective-permute-start(s16[32,640]{1,0:T(8,128)(2,1)S(1)} %sum_terms.1.refs_0_), channel_id=1, source_target_pairs={{0,4},{4,0},{8,12},{12,8},{16,20},{20,16},{24,28},{28,24},{1,5},{5... | collective-permute-start | bytes 122888 | tf_op jit(solution)/shard_map/ppermute | solution.py:334
  28.7 0.6 %collective-permute-done.4.refs_5_ = s16[32,640]{1,0:T(8,128)(2,1)S(1)} collective-permute-done((s16[32,640]{1,0:T(8,128)(2,1)S(1)}, s16[32,640]{1,0:T(8,128)(2,1)S(1)}, u32[]{:S(2)}, u32[]{:S(2)}) %collective-permute-start.4) | collective-permute-done | bytes 40992 | tf_op jit(solution)/shard_map/ppermute | solution.py:334
  29.3 0.4 collective-permute-done.3.refs_4_
  29.7 1.4 %collective-permute-done.2.refs_3_ = s16[32,640]{1,0:T(8,128)(2,1)S(1)} collective-permute-done((s16[32,640]{1,0:T(8,128)(2,1)S(1)}, s16[32,640]{1,0:T(8,128)(2,1)S(1)}, u32[]{:S(2)}, u32[]{:S(2)}) %collective-permute-start.2) | collective-permute-done | bytes 40992 | tf_op jit(solution)/shard_map/ppermute | solution.py:334
  31.0 0.3 collective-permute-done.1.refs_2_
  31.3 0.8 %collective-permute-done.refs_1_ = s16[32,640]{1,0:T(8,128)(2,1)S(1)} collective-permute-done((s16[32,640]{1,0:T(8,128)(2,1)S(1)}, s16[32,640]{1,0:T(8,128)(2,1)S(1)}, u32[]{:S(2)}, u32[]{:S(2)}) %collective-permute-start) | collective-permute-done | bytes 40992 | tf_op jit(solution)/shard_map/ppermute | solution.py:334
  32.1 9.7 %field.1 = (f32[4,640]{1,0:T(4,128)}, f32[2,4096]{1,0:T(2,128)}) custom-call(s16[640,640]{1,0:T(8,128)(2,1)S(1)} %all_gather.3.refs_0_.refs_1_.refs_2_.refs_3_.blocks_ref, f32[1,32,32]{2,1,0:T(8,128)S(1)} %copy-done.7, s32[32,128]{1,0:T(8,128)S(1)} %bitcast.6, s32[32,128]{1,0:T(8,128)S(1)} %bitcast.8, f32[2,4096]{1,0:T(2,128)S(1)} %copy-done.2, ...), custom_call_target="tpu_custom_call" | custom-call | tf_op jit(solution)/shard_map/field/pallas_call | solution.py:338
  (16 shorter events, 0.0 us)
Async XLA Ops:
  0.6 1.0 %copy-start = (f32[5,128,128]{2,1,0:T(8,128)S(1)}, f32[5,128,128]{2,1,0:T(8,128)}, u32[]{:S(2)}) copy-start(f32[5,128,128]{2,1,0:T(8,128)} %param.14) | copy-start | bytes 983044
  1.6 0.8 %copy-start.1 = (f32[2,4096]{1,0:T(2,128)S(1)}, f32[2,4096]{1,0:T(2,128)}, u32[]{:S(2)}) copy-start(f32[2,4096]{1,0:T(2,128)} %fracs_ref.3) | copy-start | bytes 98308
  2.4 0.7 %copy-start.3 = (s32[4096]{0:T(1024)S(1)}, s32[4096]{0:T(1024)}, u32[]{:S(2)}) copy-start(s32[4096]{0:T(1024)} %param.8) | copy-start | bytes 49156
  3.1 0.7 %copy-start.5 = (s32[4096]{0:T(1024)S(1)}, s32[4096]{0:T(1024)}, u32[]{:S(2)}) copy-start(s32[4096]{0:T(1024)} %param.9) | copy-start | bytes 49156
  3.8 0.7 %copy-start.8 = (f32[4096]{0:T(1024)S(1)}, f32[4096]{0:T(1024)}, u32[]{:S(2)}) copy-start(f32[4096]{0:T(1024)} %param.11) | copy-start | bytes 49156
  4.5 0.7 %copy-start.9 = (s32[4,640]{1,0:T(4,128)S(1)}, s32[4,640]{1,0:T(4,128)}, u32[]{:S(2)}) copy-start(s32[4,640]{1,0:T(4,128)} %cap_ref.1) | copy-start | bytes 30724
  5.2 0.7 %copy-start.10 = (f32[4,640]{1,0:T(4,128)S(1)}, f32[4,640]{1,0:T(4,128)}, u32[]{:S(2)}) copy-start(f32[4,640]{1,0:T(4,128)} %block_ref.1) | copy-start | bytes 30724
  17.3 14.8 %copy-start.2 = (f32[2,4096]{1,0:T(2,128)S(1)}, f32[2,4096]{1,0:T(2,128)}, u32[]{:S(2)}) copy-start(f32[2,4096]{1,0:T(2,128)} %fracs_ref.3) | copy-start | bytes 98308
  17.3 14.8 %copy-start.4 = (s32[4096]{0:T(1024)S(1)}, s32[4096]{0:T(1024)}, u32[]{:S(2)}) copy-start(s32[4096]{0:T(1024)} %param.8) | copy-start | bytes 49156
  17.3 14.8 %copy-start.6 = (s32[4096]{0:T(1024)S(1)}, s32[4096]{0:T(1024)}, u32[]{:S(2)}) copy-start(s32[4096]{0:T(1024)} %param.9) | copy-start | bytes 49156
  17.3 14.8 %copy-start.7 = (f32[1,32,32]{2,1,0:T(8,128)S(1)}, f32[1,32,32]{2,1,0:T(8,128)}, u32[]{:S(2)}) copy-start(f32[1,32,32]{2,1,0:T(8,128)} %col_blocks_ref.1) | copy-start | bytes 12292
  17.4 9.9 %collective-permute-start.6 = (s16[32,640]{1,0:T(8,128)(2,1)S(1)}, s16[32,640]{1,0:T(8,128)(2,1)S(1)}, u32[]{:S(2)}, u32[]{:S(2)}) collective-permute-start(s16[32,640]{1,0:T(8,128)(2,1)S(1)} %sum_terms.1.refs_0_), channel_id=1, source_target_pairs={{0,28},{4,24},{8,20},{12,16},{16,12},{20,8},{24,4},{28,0},{1,29},{... | collective-permute-start | bytes 122888 | tf_op jit(solution)/shard_map/ppermute | solution.py:334
  22.0 6.1 %collective-permute-start.5 = (s16[32,640]{1,0:T(8,128)(2,1)S(1)}, s16[32,640]{1,0:T(8,128)(2,1)S(1)}, u32[]{:S(2)}, u32[]{:S(2)}) collective-permute-start(s16[32,640]{1,0:T(8,128)(2,1)S(1)} %sum_terms.1.refs_0_), channel_id=1, source_target_pairs={{0,24},{4,28},{8,16},{12,20},{16,8},{20,12},{24,0},{28,4},{1,25},{... | collective-permute-start | bytes 122888 | tf_op jit(solution)/shard_map/ppermute | solution.py:334
  22.3 7.0 %collective-permute-start.4 = (s16[32,640]{1,0:T(8,128)(2,1)S(1)}, s16[32,640]{1,0:T(8,128)(2,1)S(1)}, u32[]{:S(2)}, u32[]{:S(2)}) collective-permute-start(s16[32,640]{1,0:T(8,128)(2,1)S(1)} %sum_terms.1.refs_0_), channel_id=1, source_target_pairs={{0,20},{4,16},{8,28},{12,24},{16,4},{20,0},{24,12},{28,8},{1,21},{... | collective-permute-start | bytes 122888 | tf_op jit(solution)/shard_map/ppermute | solution.py:334
  23.0 6.6 %collective-permute-start.3 = (s16[32,640]{1,0:T(8,128)(2,1)S(1)}, s16[32,640]{1,0:T(8,128)(2,1)S(1)}, u32[]{:S(2)}, u32[]{:S(2)}) collective-permute-start(s16[32,640]{1,0:T(8,128)(2,1)S(1)} %sum_terms.1.refs_0_), channel_id=1, source_target_pairs={{0,16},{4,20},{8,24},{12,28},{16,0},{20,4},{24,8},{28,12},{1,17},{... | collective-permute-start | bytes 122888 | tf_op jit(solution)/shard_map/ppermute | solution.py:334
  25.2 5.9 %collective-permute-start.2 = (s16[32,640]{1,0:T(8,128)(2,1)S(1)}, s16[32,640]{1,0:T(8,128)(2,1)S(1)}, u32[]{:S(2)}, u32[]{:S(2)}) collective-permute-start(s16[32,640]{1,0:T(8,128)(2,1)S(1)} %sum_terms.1.refs_0_), channel_id=1, source_target_pairs={{0,12},{4,8},{8,4},{12,0},{16,28},{20,24},{24,20},{28,16},{1,13},{... | collective-permute-start | bytes 122888 | tf_op jit(solution)/shard_map/ppermute | solution.py:334
  27.3 4.0 %collective-permute-start.1 = (s16[32,640]{1,0:T(8,128)(2,1)S(1)}, s16[32,640]{1,0:T(8,128)(2,1)S(1)}, u32[]{:S(2)}, u32[]{:S(2)}) collective-permute-start(s16[32,640]{1,0:T(8,128)(2,1)S(1)} %sum_terms.1.refs_0_), channel_id=1, source_target_pairs={{0,8},{4,12},{8,0},{12,4},{16,24},{20,28},{24,16},{28,20},{1,9},{5... | collective-permute-start | bytes 122888 | tf_op jit(solution)/shard_map/ppermute | solution.py:334
  28.1 4.0 %collective-permute-start = (s16[32,640]{1,0:T(8,128)(2,1)S(1)}, s16[32,640]{1,0:T(8,128)(2,1)S(1)}, u32[]{:S(2)}, u32[]{:S(2)}) collective-permute-start(s16[32,640]{1,0:T(8,128)(2,1)S(1)} %sum_terms.1.refs_0_), channel_id=1, source_target_pairs={{0,4},{4,0},{8,12},{12,8},{16,20},{20,16},{24,28},{28,24},{1,5},{5... | collective-permute-start | bytes 122888 | tf_op jit(solution)/shard_map/ppermute | solution.py:334

commit v6 on v5

--- a/solution.py
+++ b/solution.py
@@ -111,42 +111,55 @@
     out_ref[height:, :] = stored(codes)
 
 
+def beside(values):
+    width = values.shape[1]
+    lane = iota((values.shape[0], LANES), 1)
+    left, right = pltpu.roll(values, 1, 1), pltpu.roll(values, width - 1, 1)
+    first = jnp.where(lane == 0, values[:, :LANES], left[:, :LANES])
+    last = jnp.where(lane == LANES - 1, values[:, width - LANES :], right[:, width - LANES :])
+    return (
+        jnp.concatenate([first, left[:, LANES:]], 1),
+        jnp.concatenate([right[:, : width - LANES], last], 1),
+    )
+
+
 def along_lines(values):
-    width = values.shape[1]
-    column = iota(values.shape, 1)
-    left = jnp.where(column == 0, values, pltpu.roll(values, 1, 1))
-    right = jnp.where(column == width - 1, values, pltpu.roll(values, width - 1, 1))
+    left, right = beside(values)
     return 2.0 * values - left - right
 
 
 def across_lines(values):
     height = values.shape[0]
-    row = iota(values.shape, 0)
-    above = jnp.where(row == 0, values, pltpu.roll(values, 1, 0))
-    below = jnp.where(row == height - 1, values, pltpu.roll(values, height - 1, 0))
+    row = iota((8, values.shape[1]), 0)
+    above, below = pltpu.roll(values, 1, 0), pltpu.roll(values, height - 1, 0)
+    first = jnp.where(row == 0, values[:8], above[:8])
+    last = jnp.where(row == 7, values[height - 8 :], below[height - 8 :])
+    above = jnp.concatenate([first, above[8:]], 0)
+    below = jnp.concatenate([below[: height - 8], last], 0)
     return 2.0 * values - above - below
 
 
 def row_blockwise(residual, pairs_ref):
-    high, low = halves(residual)
+    count = residual.shape[0]
+    both = jnp.concatenate(halves(residual), 0)
     result = []
     for k in range(pairs_ref.shape[0]):
-        cut = slice(k * LANES, (k + 1) * LANES)
-        pair = pairs_ref[k]
-        both = last_dims(jnp.concatenate([high[:, cut], low[:, cut]], 1), jnp.concatenate([pair, pair], 1))
-        result.append(both[:, :LANES] + both[:, LANES:])
+        product = last_dims(both[:, k * LANES : (k + 1) * LANES], pairs_ref[k])
+        high, low = product[:count], product[count:]
+        result.append(high[:, :LANES] + (high[:, LANES:] + low[:, :LANES]))
     return jnp.concatenate(result, 1)
 
 
 def col_blockwise(residual, blocks):
     high, low = halves(residual)
-    count, size = len(blocks), blocks[0][0].shape[0]
+    size = blocks[0].shape[0] // 2
+    dot = functools.partial(jnp.dot, preferred_element_type=f32)
     result = []
-    for k, (block_high, block_low_part) in enumerate(blocks):
+    for k, pair in enumerate(blocks):
         cut = slice(k * size, (k + 1) * size)
-        dot = functools.partial(jnp.dot, preferred_element_type=f32)
-        result.append(dot(block_high, high[cut]) + (dot(block_low_part, high[cut]) + dot(block_high, low[cut])))
-    return result[0] if count == 1 else jnp.concatenate(result, 0)
+        both = dot(pair, high[cut])
+        result.append(both[:size] + (both[size:] + dot(pair[:size], low[cut])))
+    return result[0] if len(blocks) == 1 else jnp.concatenate(result, 0)
 
 
 def each(count, body):
@@ -209,7 +222,7 @@
             source_ref[here, cut] = term[p * chunk : (p + 1) * chunk] / weight[p * chunk : (p + 1) * chunk]
 
     lanes_at_once = width if chunks == 1 else LANES
-    col_blocks = [halves(col_blocks_ref[k]) for k in range(col_blocks_ref.shape[0])]
+    col_blocks = [jnp.concatenate(halves(col_blocks_ref[k]), 0) for k in range(col_blocks_ref.shape[0])]
     inner = pl.ds(8, height)
 
     @functools.partial(each, width // lanes_at_once)
@@ -253,9 +266,7 @@
 
     window = pltpu.roll(field_ref[pl.ds(base, 24), :], shift, 0)
     above, centre, below = window[:8], pltpu.roll(window, 23, 0)[:8], pltpu.roll(window, 22, 0)[:8]
-    column = iota(centre.shape, 1)
-    left = jnp.where(column == 0, centre, pltpu.roll(centre, 1, 1))
-    right = jnp.where(column == width - 1, centre, pltpu.roll(centre, width - 1, 1))
+    left, right = beside(centre)
     scale = jnp.maximum(centre, floor_level)
     velocity_y = rounded(-(0.5 * (below - above)) / scale)
     velocity_x = rounded(-(0.5 * (right - left)) / scale)
@@ -270,24 +281,40 @@
             stack.append(jnp.where(upper, even, pltpu.roll(odd, depth, 0)))
         return jnp.concatenate(stack, 0)
 
-    stack_y, stack_x = stacked(velocity_y), stacked(velocity_x)
-    many = stack_y.shape[0]
-    next_y = pltpu.roll(stack_y, many - depth, 0)
-    next_x = pltpu.roll(stack_x, many - depth, 0)
-    turned = [stack_y.T, next_y.T[:8], stack_x.T, next_x.T[:8]]
-    table = jnp.concatenate(turned, 0).astype(bf16)
+    half = LANES // 2
+
+    def table_of(values):
+        stack = stacked(values)
+        many = stack.shape[0]
+        blank = jnp.zeros((LANES - many, LANES), f32)
+        turned = jnp.concatenate([stack, blank], 0).T
+        after = jnp.concatenate([pltpu.roll(stack, many - depth, 0), blank], 0).T[:8]
+        return jnp.concatenate([turned[: half + 8], jnp.concatenate([turned[half:], after], 0)], 1)
+
+    table = jnp.concatenate([table_of(velocity_y), table_of(velocity_x)], 0).astype(bf16)
+    many = parts * tiles * depth
     rows, cols = rows_ref[...], cols_ref[...]
-    keys, lane = iota((many, LANES), 0), iota((LANES + 8, LANES), 0)
-    for j in range(rows.shape[0]):
-        cut = slice(j * LANES, (j + 1) * LANES)
+    joined = 2 if rows.shape[0] % 2 == 0 else 1
+    blank = jnp.zeros((LANES - many, joined * LANES), bf16)
+    keys, lane = iota((many, joined * LANES), 0), iota((half + 8, joined * LANES), 0)
+    for j in range(0, rows.shape[0], joined):
+        cut = slice(j * LANES, (j + joined) * LANES)
         fy, fx = fracs_ref[0:1, cut], fracs_ref[1:2, cut]
-        col = cols[j : j + 1]
-        key = (col >> 7) * depth + rows[j : j + 1]
-        look = pick(keys, key, rounded(1.0 - fy), rounded(fy)).astype(bf16)
-        sampled = jnp.dot(table, look, preferred_element_type=f32)
-        share = pick(lane, col & 127, rounded(1.0 - fx), rounded(fx))
-        velocity_ref[0:1, cut] = jnp.sum(sampled[: LANES + 8] * share, 0, keepdims=True)
-        velocity_ref[1:2, cut] = jnp.sum(sampled[LANES + 8 :] * share, 0, keepdims=True)
+        col = jnp.concatenate([cols[n : n + 1] for n in range(j, j + joined)], 1)
+        row = jnp.concatenate([rows[n : n + 1] for n in range(j, j + joined)], 1)
+        key = (col >> 7) * depth + row
+        second = (col & half) != 0
+        near, far = rounded(1.0 - fy), rounded(fy)
+        looks = [
+            pick(keys, jnp.where(second, -8, key), near, far).astype(bf16),
+            blank,
+            pick(keys, jnp.where(second, key, -8), near, far).astype(bf16),
+            blank,
+        ]
+        sampled = jnp.dot(table, jnp.concatenate(looks, 0), preferred_element_type=f32)
+        share = pick(lane, col & (half - 1), rounded(1.0 - fx), rounded(fx))
+        velocity_ref[0:1, cut] = jnp.sum(sampled[: half + 8] * share, 0, keepdims=True)
+        velocity_ref[1:2, cut] = jnp.sum(sampled[half + 8 :] * share, 0, keepdims=True)
 
 
 def local(pin_rows, pin_cols, pin_fracs, pin_weights, capacity, blockage, row_blocks, col_blocks):
@@ -300,6 +327,7 @@
     rows, cols = pin_rows.reshape(by_lane), pin_cols.reshape(by_lane)
     sizes = pin_weights.reshape(by_lane)
     vmem = pl.BlockSpec(memory_space=pltpu.VMEM)
+    whole = pltpu.CompilerParams(vmem_limit_bytes=60 << 20)
     small = pltpu.CompilerParams(vmem_limit_bytes=16 * 1024 * 1024)
     grid_bytes = 4 * height * width
     large = pltpu.CompilerParams(vmem_limit_bytes=(20 << 20) + 6 * grid_bytes)
@@ -310,7 +338,7 @@
         out_shape=jax.ShapeDtypeStruct((carried + LANES, width_part), jnp.int16),
         in_specs=[vmem] * 7,
         out_specs=vmem,
-        compiler_params=small,
+        compiler_params=whole,
         name="splat",
     )(rows, cols, pin_fracs, sizes, capacity, blockage, row_blocks.reshape(-1, LANES))
     blocks = lax.all_gather(terms, "cells", axis=0, tiled=True)

time: 42.4 us -> 36.8 us (0.87)
  local copies, waits for them, and re-layouts: 5.29 us -> 0.01 us
    unnamed x22 -> x8, local copies, waits for them, and re-layouts: 5.29 us -> 0.01 us
    pallas_call x1, Pallas kernels: 9.67 us -> 7.88 us  [local(): pl.pallas_call(functools.partial(field_kernel, (depth, tiles, parts, stri...]
    pallas_call x1, Pallas kernels: 1.14 us -> 2.84 us  [local(): pl.pallas_call(functools.partial(splat_kernel, tiles, parts), out_shape=j...]
where the time goes in v6:
time: 36.8 us; the launch traced here: 36.6 us
  starting transfers between devices  11.2 us (30%)
  Pallas kernels  10.8 us (29%)
  blocking collectives  10.4 us (28%)
  waiting for transfers between devices  3.47 us (9%)
  between operations  0.66 us (2%)
    ppermute x7, starting transfers between devices, local(): sent[k] = lax.ppermute(sums, 'strip', [(n, n ^ k) for n in range(strips)])  11.2 us
    all_gather x1, blocking collectives, local(): blocks = lax.all_gather(terms, 'cells', axis=0, tiled=True)  10.4 us
    pallas_call x1, Pallas kernels, local(): pl.pallas_call(functools.partial(field_kernel, (depth, tiles, parts, stri...  7.88 us
    ppermute x7, waiting for transfers between devices, local(): sent[k] = lax.ppermute(sums, 'strip', [(n, n ^ k) for n in range(strips)])  3.47 us
    pallas_call x1, Pallas kernels, local(): pl.pallas_call(functools.partial(splat_kernel, tiles, parts), out_shape=j...  2.84 us
  transfers between devices with their start and end apart: 7, of which 5 were waited for; matrix products, arithmetic and copies ran while one was open for 0% of the time, Pallas kernels for 0%

profile of v6, /device:TPU:0, one launch (start us, length us, event | category | flops | bytes accessed | tf_op | source)
XLA Modules:
  0.0 36.6 jit_solution(12025962283718424281)
XLA Ops:
  0.6 2.8 %splat.1 = s16[160,640]{1,0:T(8,128)(2,1)} custom-call(s32[32,128]{1,0:T(8,128)} %bitcast.4, s32[32,128]{1,0:T(8,128)} %bitcast.6, f32[2,4096]{1,0:T(2,128)} %fracs_ref.3, f32[32,128]{1,0:T(8,128)} %bitcast.9, s32[4,640]{1,0:T(4,128)} %cap_ref.1, f32[4,640]{1,0:T(4,128)} %block_ref.1, f32[640,128]{1,0:T(8,128)} %bitcast.8), custom_call_target="tpu_custom_call" | custom-call | tf_op jit(solution)/shard_map/splat/pallas_call | solution.py:336
  3.5 10.4 %all_gather.3.refs_0_.refs_1_.refs_2_.refs_3_.blocks_ref = s16[640,640]{1,0:T(8,128)(2,1)S(1)} all-gather(s16[160,640]{1,0:T(8,128)(2,1)} %splat.1), channel_id=1, replica_groups=mesh['strip'=8,'cells'=4] {'cells'}, dimensions={0}, use_global_device_ids=true | all-gather | bytes 1024000 | tf_op jit(solution)/shard_map/all_gather | solution.py:344
  13.9 0.0 copy-start
  13.9 0.0 copy-start.1
  13.9 0.1 sum_terms.1.refs_0_
  14.0 4.6 %collective-permute-start.6 = (s16[32,640]{1,0:T(8,128)(2,1)S(1)}, s16[32,640]{1,0:T(8,128)(2,1)S(1)}, u32[]{:S(2)}, u32[]{:S(2)}) collective-permute-start(s16[32,640]{1,0:T(8,128)(2,1)S(1)} %sum_terms.1.refs_0_), channel_id=1, source_target_pairs={{0,28},{4,24},{8,20},{12,16},{16,12},{20,8},{24,4},{28,0},{1,29},{... | collective-permute-start | bytes 122888 | tf_op jit(solution)/shard_map/ppermute | solution.py:362
  18.6 0.2 collective-permute-start.5
  18.9 0.8 %collective-permute-start.4 = (s16[32,640]{1,0:T(8,128)(2,1)S(1)}, s16[32,640]{1,0:T(8,128)(2,1)S(1)}, u32[]{:S(2)}, u32[]{:S(2)}) collective-permute-start(s16[32,640]{1,0:T(8,128)(2,1)S(1)} %sum_terms.1.refs_0_), channel_id=1, source_target_pairs={{0,20},{4,16},{8,28},{12,24},{16,4},{20,0},{24,12},{28,8},{1,21},{... | collective-permute-start | bytes 122888 | tf_op jit(solution)/shard_map/ppermute | solution.py:362
  19.6 2.1 %collective-permute-start.3 = (s16[32,640]{1,0:T(8,128)(2,1)S(1)}, s16[32,640]{1,0:T(8,128)(2,1)S(1)}, u32[]{:S(2)}, u32[]{:S(2)}) collective-permute-start(s16[32,640]{1,0:T(8,128)(2,1)S(1)} %sum_terms.1.refs_0_), channel_id=1, source_target_pairs={{0,16},{4,20},{8,24},{12,28},{16,0},{20,4},{24,8},{28,12},{1,17},{... | collective-permute-start | bytes 122888 | tf_op jit(solution)/shard_map/ppermute | solution.py:362
  21.8 2.2 %collective-permute-start.2 = (s16[32,640]{1,0:T(8,128)(2,1)S(1)}, s16[32,640]{1,0:T(8,128)(2,1)S(1)}, u32[]{:S(2)}, u32[]{:S(2)}) collective-permute-start(s16[32,640]{1,0:T(8,128)(2,1)S(1)} %sum_terms.1.refs_0_), channel_id=1, source_target_pairs={{0,12},{4,8},{8,4},{12,0},{16,28},{20,24},{24,20},{28,16},{1,13},{... | collective-permute-start | bytes 122888 | tf_op jit(solution)/shard_map/ppermute | solution.py:362
  23.9 0.0 collective-permute-done.6.refs_7_
  23.9 0.8 %collective-permute-start.1 = (s16[32,640]{1,0:T(8,128)(2,1)S(1)}, s16[32,640]{1,0:T(8,128)(2,1)S(1)}, u32[]{:S(2)}, u32[]{:S(2)}) collective-permute-start(s16[32,640]{1,0:T(8,128)(2,1)S(1)} %sum_terms.1.refs_0_), channel_id=1, source_target_pairs={{0,8},{4,12},{8,0},{12,4},{16,24},{20,28},{24,16},{28,20},{1,9},{5... | collective-permute-start | bytes 122888 | tf_op jit(solution)/shard_map/ppermute | solution.py:362
  24.7 0.0 collective-permute-done.5.refs_6_
  24.7 0.5 %collective-permute-start = (s16[32,640]{1,0:T(8,128)(2,1)S(1)}, s16[32,640]{1,0:T(8,128)(2,1)S(1)}, u32[]{:S(2)}, u32[]{:S(2)}) collective-permute-start(s16[32,640]{1,0:T(8,128)(2,1)S(1)} %sum_terms.1.refs_0_), channel_id=1, source_target_pairs={{0,4},{4,0},{8,12},{12,8},{16,20},{20,16},{24,28},{28,24},{1,5},{5... | collective-permute-start | bytes 122888 | tf_op jit(solution)/shard_map/ppermute | solution.py:362
  25.3 0.6 %collective-permute-done.4.refs_5_ = s16[32,640]{1,0:T(8,128)(2,1)S(1)} collective-permute-done((s16[32,640]{1,0:T(8,128)(2,1)S(1)}, s16[32,640]{1,0:T(8,128)(2,1)S(1)}, u32[]{:S(2)}, u32[]{:S(2)}) %collective-permute-start.4) | collective-permute-done | bytes 40992 | tf_op jit(solution)/shard_map/ppermute | solution.py:362
  25.9 0.4 collective-permute-done.3.refs_4_
  26.3 1.4 %collective-permute-done.2.refs_3_ = s16[32,640]{1,0:T(8,128)(2,1)S(1)} collective-permute-done((s16[32,640]{1,0:T(8,128)(2,1)S(1)}, s16[32,640]{1,0:T(8,128)(2,1)S(1)}, u32[]{:S(2)}, u32[]{:S(2)}) %collective-permute-start.2) | collective-permute-done | bytes 40992 | tf_op jit(solution)/shard_map/ppermute | solution.py:362
  27.6 0.3 collective-permute-done.1.refs_2_
  27.9 0.8 %collective-permute-done.refs_1_ = s16[32,640]{1,0:T(8,128)(2,1)S(1)} collective-permute-done((s16[32,640]{1,0:T(8,128)(2,1)S(1)}, s16[32,640]{1,0:T(8,128)(2,1)S(1)}, u32[]{:S(2)}, u32[]{:S(2)}) %collective-permute-start) | collective-permute-done | bytes 40992 | tf_op jit(solution)/shard_map/ppermute | solution.py:362
  28.7 0.0 copy-done
  28.7 0.0 copy-done.1
  28.7 0.0 copy-done.2
  28.7 0.0 copy-done.3
  28.7 7.9 %field.1 = (f32[4,640]{1,0:T(4,128)}, f32[2,4096]{1,0:T(2,128)}) custom-call(s16[640,640]{1,0:T(8,128)(2,1)S(1)} %all_gather.3.refs_0_.refs_1_.refs_2_.refs_3_.blocks_ref, f32[1,32,32]{2,1,0:T(8,128)S(1)} %copy-done.3, s32[32,128]{1,0:T(8,128)S(1)} %bitcast.5, s32[32,128]{1,0:T(8,128)S(1)} %bitcast.7, f32[2,4096]{1,0:T(2,128)S(1)} %copy-done, ...), custom_call_target="tpu_custom_call" | custom-call | tf_op jit(solution)/shard_map/field/pallas_call | solution.py:366
  (2 shorter events, 0.0 us)
Async XLA Ops:
  13.9 14.8 %copy-start = (f32[2,4096]{1,0:T(2,128)S(1)}, f32[2,4096]{1,0:T(2,128)}, u32[]{:S(2)}) copy-start(f32[2,4096]{1,0:T(2,128)} %fracs_ref.3) | copy-start | bytes 98308
  13.9 14.8 %copy-start.1 = (s32[4096]{0:T(1024)S(1)}, s32[4096]{0:T(1024)}, u32[]{:S(2)}) copy-start(s32[4096]{0:T(1024)} %param.8) | copy-start | bytes 49156
  13.9 14.8 %copy-start.2 = (s32[4096]{0:T(1024)S(1)}, s32[4096]{0:T(1024)}, u32[]{:S(2)}) copy-start(s32[4096]{0:T(1024)} %param.9) | copy-start | bytes 49156
  13.9 14.8 %copy-start.3 = (f32[1,32,32]{2,1,0:T(8,128)S(1)}, f32[1,32,32]{2,1,0:T(8,128)}, u32[]{:S(2)}) copy-start(f32[1,32,32]{2,1,0:T(8,128)} %col_blocks_ref.1) | copy-start | bytes 12292
  14.0 9.9 %collective-permute-start.6 = (s16[32,640]{1,0:T(8,128)(2,1)S(1)}, s16[32,640]{1,0:T(8,128)(2,1)S(1)}, u32[]{:S(2)}, u32[]{:S(2)}) collective-permute-start(s16[32,640]{1,0:T(8,128)(2,1)S(1)} %sum_terms.1.refs_0_), channel_id=1, source_target_pairs={{0,28},{4,24},{8,20},{12,16},{16,12},{20,8},{24,4},{28,0},{1,29},{... | collective-permute-start | bytes 122888 | tf_op jit(solution)/shard_map/ppermute | solution.py:362
  18.6 6.1 %collective-permute-start.5 = (s16[32,640]{1,0:T(8,128)(2,1)S(1)}, s16[32,640]{1,0:T(8,128)(2,1)S(1)}, u32[]{:S(2)}, u32[]{:S(2)}) collective-permute-start(s16[32,640]{1,0:T(8,128)(2,1)S(1)} %sum_terms.1.refs_0_), channel_id=1, source_target_pairs={{0,24},{4,28},{8,16},{12,20},{16,8},{20,12},{24,0},{28,4},{1,25},{... | collective-permute-start | bytes 122888 | tf_op jit(solution)/shard_map/ppermute | solution.py:362
  18.9 7.0 %collective-permute-start.4 = (s16[32,640]{1,0:T(8,128)(2,1)S(1)}, s16[32,640]{1,0:T(8,128)(2,1)S(1)}, u32[]{:S(2)}, u32[]{:S(2)}) collective-permute-start(s16[32,640]{1,0:T(8,128)(2,1)S(1)} %sum_terms.1.refs_0_), channel_id=1, source_target_pairs={{0,20},{4,16},{8,28},{12,24},{16,4},{20,0},{24,12},{28,8},{1,21},{... | collective-permute-start | bytes 122888 | tf_op jit(solution)/shard_map/ppermute | solution.py:362
  19.6 6.6 %collective-permute-start.3 = (s16[32,640]{1,0:T(8,128)(2,1)S(1)}, s16[32,640]{1,0:T(8,128)(2,1)S(1)}, u32[]{:S(2)}, u32[]{:S(2)}) collective-permute-start(s16[32,640]{1,0:T(8,128)(2,1)S(1)} %sum_terms.1.refs_0_), channel_id=1, source_target_pairs={{0,16},{4,20},{8,24},{12,28},{16,0},{20,4},{24,8},{28,12},{1,17},{... | collective-permute-start | bytes 122888 | tf_op jit(solution)/shard_map/ppermute | solution.py:362
  21.8 5.9 %collective-permute-start.2 = (s16[32,640]{1,0:T(8,128)(2,1)S(1)}, s16[32,640]{1,0:T(8,128)(2,1)S(1)}, u32[]{:S(2)}, u32[]{:S(2)}) collective-permute-start(s16[32,640]{1,0:T(8,128)(2,1)S(1)} %sum_terms.1.refs_0_), channel_id=1, source_target_pairs={{0,12},{4,8},{8,4},{12,0},{16,28},{20,24},{24,20},{28,16},{1,13},{... | collective-permute-start | bytes 122888 | tf_op jit(solution)/shard_map/ppermute | solution.py:362
  23.9 4.0 %collective-permute-start.1 = (s16[32,640]{1,0:T(8,128)(2,1)S(1)}, s16[32,640]{1,0:T(8,128)(2,1)S(1)}, u32[]{:S(2)}, u32[]{:S(2)}) collective-permute-start(s16[32,640]{1,0:T(8,128)(2,1)S(1)} %sum_terms.1.refs_0_), channel_id=1, source_target_pairs={{0,8},{4,12},{8,0},{12,4},{16,24},{20,28},{24,16},{28,20},{1,9},{5... | collective-permute-start | bytes 122888 | tf_op jit(solution)/shard_map/ppermute | solution.py:362
  24.7 4.0 %collective-permute-start = (s16[32,640]{1,0:T(8,128)(2,1)S(1)}, s16[32,640]{1,0:T(8,128)(2,1)S(1)}, u32[]{:S(2)}, u32[]{:S(2)}) collective-permute-start(s16[32,640]{1,0:T(8,128)(2,1)S(1)} %sum_terms.1.refs_0_), channel_id=1, source_target_pairs={{0,4},{4,0},{8,12},{12,8},{16,20},{20,16},{24,28},{28,24},{1,5},{5... | collective-permute-start | bytes 122888 | tf_op jit(solution)/shard_map/ppermute | solution.py:362
